TPU v7x, 512 devices: a whole 4x8x8 slice. The times are simulated.
512 devices in a mesh: seq: 64 (over y, z_hi, core), dp: 8 (over x, z_lo).
Axes of the slice: x: 4, y: 8, z: 8 (z_hi: 4, z_lo: 2; z = z_hi * 2 + z_lo), core: 2. Of those that a mesh axis runs over, the one named last changes fastest.
Arguments:
- inputs: bfloat16 [8, 16384, 2048], P('dp', 'seq'), may hold values from -6 to 6
- short_filters: float32 [3, 3, 2048], replicated, may hold values from -3.5 to 3.5
- long_filter: float32 [128, 128], replicated, may hold values from -2 to 2
- grad_out: bfloat16 [8, 16384, 2048], P('dp', 'seq'), may hold values from -6 to 6
Outputs:
- grad_in: bfloat16 [8, 16384, 2048], P('dp', 'seq')
- grad_short: float32 [3, 3, 2048], replicated
- grad_long: float32 [128, 128], replicated
All inputs are finite; a program needn't handle non-finite values.
Results may differ from a plain program's by a relative error of at most 0.0058.
Values may be sent and summed in bfloat16 or wider, within the bound.
No kernel may reach another device: no remote copies, remote signals or barrier semaphores. Data moves between devices by JAX's collectives and lax.ppermute only.
A program may use at most 192 MiB of HBM per device.

v0:
```python
import math

import jax
import jax.numpy as jnp
from jax import lax
from jax.sharding import PartitionSpec as P


def from_behind(shard, axis, by):
    size = lax.axis_size(axis)
    pairs = [(i, i + by) for i in range(size) if 0 <= i + by < size]
    return lax.ppermute(shard, axis, pairs)


def to_grouped(values, group_count):
    lead = values.shape[:-1]
    width = values.shape[-1] // group_count
    return jnp.swapaxes(values.reshape(lead + (group_count, width)), -1, -2).reshape(values.shape)


def from_grouped(values, group_count):
    lead = values.shape[:-1]
    width = values.shape[-1] // group_count
    return jnp.swapaxes(values.reshape(lead + (width, group_count)), -1, -2).reshape(values.shape)


def short_apply(extended, filters):
    row_count = extended.shape[1] - 2
    return (
        filters[0] * extended[:, 2:]
        + filters[1] * extended[:, 1 : row_count + 1]
        + filters[2] * extended[:, :row_count]
    )


def toeplitz_tables(long_filter, tap_count):
    group_count = long_filter.shape[0]
    coarse = long_filter.astype(jnp.bfloat16)
    period = 2 * tap_count + 1
    padded = jnp.concatenate(
        [
            jnp.zeros((group_count, 1), jnp.bfloat16),
            coarse[:, ::-1],
            jnp.zeros((group_count, tap_count), jnp.bfloat16),
        ],
        axis=1,
    )
    tiled = jnp.tile(padded, (1, tap_count))[:, : tap_count * (period - 1)].reshape(
        group_count, tap_count, period - 1
    )
    return (tiled[:, :, :tap_count], tiled[:, :, tap_count:])


def local(inputs, short_filters, long_filter, grad_out):
    seq_count, row_count, chan_count = inputs.shape
    group_count, tap_count = long_filter.shape
    group_width = chan_count // group_count
    block_count = row_count // tap_count
    block_shape = (seq_count, block_count, tap_count, group_width, group_count)
    inputs = to_grouped(inputs, group_count)
    grad_out = to_grouped(grad_out, group_count)
    short_filters = to_grouped(short_filters, group_count)
    table_prev, table_here = toeplitz_tables(long_filter, tap_count)
    as_float = inputs.astype(jnp.float32)
    zero_rows = jnp.zeros((seq_count, 2, chan_count), jnp.float32)
    local_ext = jnp.concatenate([zero_rows, as_float], axis=1)
    key_local = short_apply(local_ext, short_filters[1])
    value_local = short_apply(local_ext, short_filters[2])
    prod_local = (key_local * value_local).astype(jnp.bfloat16)
    input_prev, product_prev = from_behind(
        (inputs[:, row_count - 2 :], prod_local[:, row_count - tap_count :]), "seq", 1
    )
    prev_float = input_prev.astype(jnp.float32)
    extended = jnp.concatenate([prev_float, as_float], axis=1)
    rim_input = jnp.concatenate([prev_float, zero_rows], axis=1)
    query = short_apply(extended, short_filters[0])
    key_part = key_local.at[:, :2].add(short_apply(rim_input, short_filters[1]))
    value_part = value_local.at[:, :2].add(short_apply(rim_input, short_filters[2]))
    leading = (key_part[:, :2] * value_part[:, :2]).astype(jnp.bfloat16)
    product = jnp.concatenate([leading, prod_local[:, 2:]], axis=1)
    current = product.reshape(block_shape)
    previous = jnp.concatenate([product_prev, product[:, : row_count - tap_count]], axis=1).reshape(
        block_shape
    )
    convolved = jnp.einsum(
        "gij,snjkg->snikg", table_here, current, preferred_element_type=jnp.float32
    )
    convolved = convolved + jnp.einsum(
        "gij,snjkg->snikg", table_prev, previous, preferred_element_type=jnp.float32
    )
    convolved = convolved.reshape(seq_count, row_count, chan_count)
    cotangent = grad_out.astype(jnp.float32)
    grad_conv = (cotangent * query).astype(jnp.bfloat16)
    grad_query = cotangent * convolved
    grad_blocks = grad_conv.reshape(block_shape)
    backward = jnp.einsum(
        "gij,snikg->snjkg", table_here, grad_blocks, preferred_element_type=jnp.float32
    )
    following = from_behind(grad_conv[:, :tap_count], "seq", -1)
    after_blocks = jnp.concatenate([grad_conv[:, tap_count:], following], axis=1).reshape(
        block_shape
    )
    backward = backward + jnp.einsum(
        "gij,snikg->snjkg", table_prev, after_blocks, preferred_element_type=jnp.float32
    )
    grad_prod = backward.reshape(seq_count, row_count, chan_count)
    grad_key = grad_prod * value_part
    grad_value = grad_prod * key_part
    stacked = jnp.stack([grad_query, grad_key, grad_value])
    next_rows = from_behind(stacked[:, :, :2].astype(jnp.bfloat16), "seq", -1).astype(jnp.float32)
    extended_grads = jnp.concatenate([stacked, next_rows], axis=2)
    total = jnp.zeros((seq_count, row_count, chan_count), jnp.float32)
    for lag_index in range(3):
        total = total + jnp.sum(
            short_filters[:, lag_index][:, None, None, :]
            * extended_grads[:, :, lag_index : lag_index + row_count],
            axis=0,
        )
    grad_in = from_grouped(total.astype(jnp.bfloat16), group_count)
    token_total = row_count * seq_count * lax.axis_size("seq") * lax.axis_size("dp")
    grad_scale = 1.0 / math.sqrt(token_total)
    columns = []
    for lag_index in range(3):
        offset_rows = 2 - lag_index
        columns.append(
            jnp.sum(stacked * extended[None, :, offset_rows : offset_rows + row_count], axis=(1, 2))
        )
    grad_short = from_grouped(jnp.stack(columns, axis=1), group_count) * grad_scale
    window = jnp.concatenate([previous, current], axis=2)
    moments = jnp.einsum(
        "snikg,snjkg->gij", grad_blocks, window, preferred_element_type=jnp.float32
    )
    flattened = moments.reshape(group_count, 2 * tap_count * tap_count)
    padded = jnp.concatenate([flattened, jnp.zeros((group_count, tap_count), jnp.float32)], axis=1)
    padded = padded.reshape(group_count, tap_count, 2 * tap_count + 1)
    grad_long = jnp.sum(padded[:, :, 1 : tap_count + 1], axis=1)[:, ::-1] * grad_scale
    grad_short, grad_long = lax.psum((grad_short, grad_long), ("seq", "dp"))
    return (grad_in, grad_short, grad_long)


def solution(mesh):
    in_specs = (P("dp", "seq", None), P(), P(), P("dp", "seq", None))
    out_specs = (P("dp", "seq", None), P(), P())
    return jax.shard_map(local, mesh=mesh, in_specs=in_specs, out_specs=out_specs, check_vma=False)
```

profile of v0, /device:TPU:1, one launch (start us, length us, event | category | flops | bytes accessed | tf_op | source)
XLA Modules:
  0.0 499.6 jit_solution(7844540235305831345)
XLA Ops:
  7.2 1.5 copy.141
  10.7 7.2 %collective-permute-start = (bf16[1,2,2048]{2,1,0:T(2,128)(2,1)}, bf16[1,2,2048]{2,1,0:T(2,128)(2,1)}, u32[]{:S(2)}, u32[]{:S(2)}) collective-permute-start(bf16[1,2,2048]{2,1,0:T(2,128)(2,1)} %slice.215), channel_id=1, source_target_pairs={{0,8},{8,16},{16,24},{24,32},{32,40},{40,48},{48,56},{56,64},{64,7... | collective-permute-start | bytes 24584 | tf_op jit(solution)/shard_map/ppermute | solution.py:12
  17.9 1.5 convert_element_type.127
  20.4 1.8 fusion.27
  25.1 3.0 multiply_convert_fusion.1
  30.0 1.9 collective-permute-start.1
  34.9 2.3 copy.138
  37.2 2.9 convert_bitcast_fusion
  40.1 4.5 tile.4
  44.5 12.9 %tile.10 = bf16[128,32896]{0,1:T(8,128)(2,1)} reshape(bf16[128,128,257]{0,2,1:T(8,128)(2,1)} %tile.4) | data formatting | bytes 16842752 | tf_op jit(solution)/shard_map/tile | solution.py:48
  57.4 3.4 slice-done
  60.8 3.9 fusion.25
  64.7 1.7 copy.172
  66.9 2.9 copy.173
  69.8 4.1 copy.139
  73.9 2.9 copy.155
  76.9 2.9 copy.168
  79.8 6.7 %copy.189 = bf16[128,128,128]{2,1,0:T(8,128)(2,1)} copy(bf16[128,128,128]{0,2,1:T(8,128)(2,1)} %get-tuple-element.53) | data formatting | bytes 8388608
  86.5 6.8 %copy.190 = bf16[128,128,128]{2,1,0:T(8,128)(2,1)} copy(bf16[128,128,128]{0,2,1:T(8,128)(2,1)} %get-tuple-element.54) | data formatting | bytes 8388608
  96.5 3.2 copy.176
  99.7 3.2 copy.152
  105.1 2.3 copy.175
  107.4 2.2 copy.153
  109.6 4.9 fusion.4
  114.6 3.6 add_bitcast_fusion.1
  118.2 3.3 copy.154
  121.5 4.6 fusion.14
  128.4 2.5 copy.161
  130.9 3.6 collective-permute-start.2
  134.5 8.1 %convolution_bitcast_fusion = f32[128,128,256]{2,1,0:T(8,128)} fusion(bf16[2,128,16,128]{1,2,0,3:T(8,128)(2,1)S(1)} %copy.161, bf16[1,2,128,16,128]{2,3,1,4,0:T(8,128)(2,1)S(1)} %copy-done.13, bf16[1,2,128,16,128]{2,3,1,4,0:T(8,128)(2,1)S(1)} %copy-done.14), kind=kOutput, calls=%fused_computation | convolution fusion | flops 272629760 | bytes 19922944 | tf_op jit(solution)/shard_map/snikg,snjkg->gij/dot_general | solution.py:130
  142.6 17.8 %copy.185 = f32[128,128,256]{0,2,1:T(8,128)} copy(f32[128,128,256]{2,1,0:T(8,128)} %convolution_bitcast_fusion) | data formatting | bytes 33554432 | tf_op jit(solution)/shard_map/reshape | solution.py:133
  160.5 13.3 %concatenate.76 = f32[128,32896]{0,1:T(8,128)} pad(f32[128,32768]{0,1:T(8,128)} %bitcast.142, f32[]{:T(128)} %constant.53.clone.1), padding=0_0x0_128 | pad | bytes 33619972 | tf_op jit(solution)/shard_map/concatenate | solution.py:134
  173.8 17.5 %reshape.691 = f32[128,128,257]{0,2,1:T(8,128)} reshape(f32[128,32896]{0,1:T(8,128)} %concatenate.76) | data formatting | bytes 33685504 | tf_op jit(solution)/shard_map/reshape | solution.py:135
  191.2 4.6 slice_reduce_fusion
  196.5 4.1 copy_multiply_fusion
  201.9 1.5 copy.162
  203.5 3.5 fusion.2
  208.3 2.2 copy.163
  210.5 4.3 multiply_bitcast_fusion.1
  215.8 3.5 multiply_reduce_fusion.2
  219.4 1.9 collective-permute-start.3
  222.6 4.0 collective-permute-done.3
  226.6 2.7 pad_maximum_fusion
  229.3 2.4 fusion.1
  233.5 1.4 copy.179
  234.9 254.7 %all-reduce.6.cloned.1.call-done = (f32[3,3,2048]{2,1,0:T(4,128)}, f32[128,128]{0,1:T(8,128)}) async-done(((f32[3,3,2048]{2,1,0:T(4,128)}, f32[128,128]{0,1:T(8,128)}), (f32[3,3,2048]{2,1,0:T(4,128)}, f32[128,128]{0,1:T(8,128)})) %all-reduce.6.cloned.1.call-update) | async-done | bytes 139280 | tf_op jit(solution)/shard_map/psum | solution.py:137
  489.6 1.6 copy.180
  491.2 1.5 copy.220
  (121 shorter events, 26.2 us)
Async XLA Ops:
  7.2 482.4 %all-reduce.6.cloned.1.call-start = ((), (), s32[]{:S(2)}) async-start(), calls=%async_computation | async-start | bytes 327680 | tf_op jit(solution)/shard_map/psum | solution.py:137
  9.7 1.0 copy-start.12
  9.7 9.6 %copy-start.19 = (f32[3,3,2048]{2,1,0:T(4,128)S(1)}, f32[3,3,2048]{2,1,0:T(4,128)}, u32[]{:S(2)}) copy-start(f32[3,3,2048]{2,1,0:T(4,128)} %param.9) | copy-start | bytes 221188
  10.7 82.6 %collective-permute-start = (bf16[1,2,2048]{2,1,0:T(2,128)(2,1)}, bf16[1,2,2048]{2,1,0:T(2,128)(2,1)}, u32[]{:S(2)}, u32[]{:S(2)}) collective-permute-start(bf16[1,2,2048]{2,1,0:T(2,128)(2,1)} %slice.215), channel_id=1, source_target_pairs={{0,8},{8,16},{16,24},{24,32},{32,40},{40,48},{48,56},{56,64},{64,7... | collective-permute-start | bytes 24584 | tf_op jit(solution)/shard_map/ppermute | solution.py:12
  23.1 5.1 %copy-start.26 = (f32[1,1,16,128]{3,2,1,0:T(8,128)}, f32[1,1,16,128]{3,2,1,0:T(8,128)S(1)}, u32[]{:S(2)}) copy-start(f32[1,1,16,128]{3,2,1,0:T(8,128)S(1)} %copy.147) | copy-start | bytes 24580
  25.0 3.2 copy-start.20
  25.0 3.1 copy-start.22
  25.1 3.1 copy-start.24
  25.1 8.8 %copy-start.28 = (f32[128,128]{1,0:T(8,128)S(1)}, f32[128,128]{1,0:T(8,128)}, u32[]{:S(2)}) copy-start(f32[128,128]{1,0:T(8,128)} %param.10) | copy-start | bytes 196612
  28.2 1.0 copy-start.10
  30.0 73.7 %collective-permute-start.1 = (bf16[1,128,2048]{2,1,0:T(8,128)(2,1)}, bf16[1,128,2048]{2,1,0:T(8,128)(2,1)}, u32[]{:S(2)}, u32[]{:S(2)}) collective-permute-start(bf16[1,128,2048]{2,1,0:T(8,128)(2,1)} %slice.223), channel_id=1, source_target_pairs={{0,8},{8,16},{16,24},{24,32},{32,40},{40,48},{48,56},{56,64},{64,7... | collective-permute-start | bytes 1572872 | tf_op jit(solution)/shard_map/ppermute | solution.py:12
  57.4 3.4 slice-start
  60.8 3.9 copy-start.18
  60.8 3.9 copy-start.27
  64.6 1.8 copy-start.11
  64.7 2.0 copy-start.17
  86.5 7.5 %copy-start.21 = (f32[1,1,16,128]{3,2,1,0:T(8,128)S(1)}, f32[1,1,16,128]{3,2,1,0:T(8,128)}, u32[]{:S(2)}) copy-start(f32[1,1,16,128]{3,2,1,0:T(8,128)} %copy-done.20) | copy-start | bytes 24580
  86.5 7.5 %copy-start.23 = (f32[1,1,16,128]{3,2,1,0:T(8,128)S(1)}, f32[1,1,16,128]{3,2,1,0:T(8,128)}, u32[]{:S(2)}) copy-start(f32[1,1,16,128]{3,2,1,0:T(8,128)} %copy-done.22) | copy-start | bytes 24580
  86.5 7.5 %copy-start.25 = (f32[1,1,16,128]{3,2,1,0:T(8,128)S(1)}, f32[1,1,16,128]{3,2,1,0:T(8,128)}, u32[]{:S(2)}) copy-start(f32[1,1,16,128]{3,2,1,0:T(8,128)} %copy-done.24) | copy-start | bytes 24580
  86.5 7.5 %copy-start.29 = (f32[2048]{0:T(1024)S(1)}, f32[2048]{0:T(1024)}, u32[]{:S(2)}) copy-start(f32[2048]{0:T(1024)} %broadcast_multiply_fusion.2) | copy-start | bytes 24580
  109.6 4.9 copy-start
  109.6 4.9 copy-start.15
  127.2 7.3 %copy-start.13 = (bf16[1,2,128,16,128]{2,3,1,4,0:T(8,128)(2,1)S(1)}, bf16[1,2,128,16,128]{2,3,1,4,0:T(8,128)(2,1)}, u32[]{:S(2)}) copy-start(bf16[1,2,128,16,128]{2,3,1,4,0:T(8,128)(2,1)} %copy.176) | copy-start | bytes 3145732
  127.2 7.3 %copy-start.14 = (bf16[1,2,128,16,128]{2,3,1,4,0:T(8,128)(2,1)S(1)}, bf16[1,2,128,16,128]{2,3,1,4,0:T(8,128)(2,1)}, u32[]{:S(2)}) copy-start(bf16[1,2,128,16,128]{2,3,1,4,0:T(8,128)(2,1)} %copy.175) | copy-start | bytes 3145732
  130.9 69.7 %collective-permute-start.2 = (bf16[1,128,2048]{2,1,0:T(8,128)(2,1)}, bf16[1,128,2048]{2,1,0:T(8,128)(2,1)}, u32[]{:S(2)}, u32[]{:S(2)}) collective-permute-start(bf16[1,128,2048]{2,1,0:T(8,128)(2,1)} %get-tuple-element.62), channel_id=1, source_target_pairs={{8,0},{16,8},{24,16},{32,24},{40,32},{48,40},{56,48},{64,56},{72,6... | collective-permute-start | bytes 1572872 | tf_op jit(solution)/shard_map/ppermute | solution.py:12
  191.2 5.2 %copy-start.4 = (f32[1,2,128,16,128]{4,3,0,2,1:T(8,128)S(1)}, f32[1,2,128,16,128]{4,3,0,2,1:T(8,128)}, u32[]{:S(2)}) copy-start(f32[1,2,128,16,128]{4,3,0,2,1:T(8,128)} %copy.154) | copy-start | bytes 6291460
  196.5 4.1 copy-start.16
  203.4 3.6 copy-start.1
  210.5 4.3 copy-start.6
  210.5 4.3 copy-start.7
  210.5 4.7 copy-start.8
  210.5 5.3 %copy-start.9 = (f32[1,1,256,2048]{3,2,1,0:T(8,128)S(1)}, f32[1,1,256,2048]{3,2,1,0:T(8,128)}, u32[]{:S(2)}) copy-start(f32[1,1,256,2048]{3,2,1,0:T(8,128)} %get-tuple-element.58) | copy-start | bytes 6291460
  214.8 4.5 copy-start.2
  215.8 3.5 copy-start.3
  219.4 7.2 %collective-permute-start.3 = (bf16[3,1,2,2048]{3,2,1,0:T(2,128)(2,1)S(1)}, bf16[3,1,2,2048]{3,2,1,0:T(2,128)(2,1)S(1)}, u32[]{:S(2)}, u32[]{:S(2)}) collective-permute-start(bf16[3,1,2,2048]{3,2,1,0:T(2,128)(2,1)S(1)} %fusion.23), channel_id=1, source_target_pairs={{8,0},{16,8},{24,16},{32,24},{40,32},{48,40},{56,48},{64,56},{72,6... | collective-permute-start | bytes 73736 | tf_op jit(solution)/shard_map/ppermute | solution.py:12
  229.3 2.4 copy-start.5
Sparse Core Ops, SparseCore 0:
  222.7 266.8 all-reduce.5
where the time goes:
time: 502 us; the launch traced here: 500 us
  waiting for transfers between devices  259 us (52%)
  local copies, waits for them, and re-layouts  150 us (30%)
  other arithmetic  39.8 us (8%)
  matrix products  21.5 us (4%)
  starting transfers between devices  14.7 us (3%)
  between operations  14.5 us (3%)
    psum x1, waiting for transfers between devices, local(): grad_short, grad_long = lax.psum((grad_short, grad_long), ('seq', 'dp'))  255 us
    unnamed x76, local copies, waits for them, and re-layouts  27.2 us
    reshape x1, local copies, waits for them, and re-layouts, local(): flattened = moments.reshape(group_count, 2 * tap_count * tap_count)  17.8 us
    reshape x1, local copies, waits for them, and re-layouts, local(): padded = padded.reshape(group_count, tap_count, 2 * tap_count + 1)  17.5 us
    another operation x2, local copies, waits for them, and re-layouts, toeplitz_tables(): jnp.tile(padded, (1, tap_count))[:, :tap_count * (period - 1)]  17.3 us
    ppermute x4, starting transfers between devices, from_behind(): return lax.ppermute(shard, axis, pairs)  14.6 us
    concatenate x1, local copies, waits for them, and re-layouts, local(): jnp.concatenate([flattened, jnp.zeros((group_count, tap_count), jnp.float...  13.3 us
  transfers between devices with their start and end apart: 5, of which 2 were waited for; matrix products, arithmetic and copies ran while one was open for 31% of the time, Pallas kernels for 0%

commit v1 on v0

v1 whole, which is shorter than its diff:
```python
import functools
import math

import jax
import jax.numpy as jnp
from jax import lax
from jax.experimental import pallas as pl
from jax.experimental.pallas import tpu as pltpu
from jax.sharding import Mesh, PartitionSpec as P

F32 = jnp.float32
BF16 = jnp.bfloat16
LANES = 128
EDGE = 16
PIECE = 32


def taps_of(filt_ref, branch, lo, hi):
    return [filt_ref[3 * branch + lag : 3 * branch + lag + 1, lo:hi] for lag in range(3)]


def shorten(taps, rows_at):
    return taps[0] * rows_at(0) + taps[1] * rows_at(1) + taps[2] * rows_at(2)


def edge_kernel(x_ref, g_ref, filt_ref, ahead_ref, behind_ref, ext):
    rows, width = x_ref.shape
    taps = ahead_ref.shape[0] - EDGE
    ext[0:8, :] = jnp.zeros((8, width), F32)
    ext[8:, :] = x_ref[...].astype(F32)
    query_taps, key_taps, value_taps = (taps_of(filt_ref, i, 0, width) for i in range(3))
    for start in range(0, taps, PIECE):
        tail = rows - taps + start
        at = lambda lag: ext[8 + tail - lag : 8 + tail - lag + PIECE, :]
        product = shorten(key_taps, at) * shorten(value_taps, at)
        ahead_ref[start : start + PIECE, :] = product.astype(BF16)
        at = lambda lag: ext[8 + start - lag : 8 + start - lag + PIECE, :]
        query = shorten(query_taps, at)
        grad = g_ref[start : start + PIECE, :].astype(F32) * query
        behind_ref[start : start + PIECE, :] = grad.astype(BF16)
    ahead_ref[taps:, :] = x_ref[rows - EDGE :, :]
    behind_ref[taps : taps + EDGE, :] = x_ref[:EDGE, :]
    behind_ref[taps + EDGE :, :] = g_ref[:EDGE, :]


def edge_call(x, g, filt, taps, width):
    rows, chans = x.shape
    whole = lambda r: pl.BlockSpec((r, width), lambda i: (0, i))
    return pl.pallas_call(
        edge_kernel,
        grid=(chans // width,),
        in_specs=[whole(rows), whole(rows), whole(filt.shape[0])],
        out_specs=[whole(taps + EDGE), whole(taps + 2 * EDGE)],
        out_shape=[
            jax.ShapeDtypeStruct((taps + EDGE, chans), BF16),
            jax.ShapeDtypeStruct((taps + 2 * EDGE, chans), BF16),
        ],
        scratch_shapes=[pltpu.VMEM((rows + 8, width), F32)],
        name="edges",
    )(x, g, filt)


def table_kernel(coarse_ref, turned_ref, fwd_ref, bwd_ref):
    taps = coarse_ref.shape[1]
    row = lax.broadcasted_iota(jnp.int32, (taps, taps), 0)
    col = lax.broadcasted_iota(jnp.int32, (taps, taps), 1)
    for j in range(coarse_ref.shape[0]):
        at = slice(j * taps, (j + 1) * taps)
        circ = jnp.broadcast_to(turned_ref[j : j + 1, :], (taps, taps))
        circ = pltpu.roll(circ, 0, 1, stride=1, stride_axis=0)
        fwd_ref[at, :taps] = jnp.where(col > row, circ, 0.0).astype(BF16)
        fwd_ref[at, taps:] = jnp.where(col <= row, circ, 0.0).astype(BF16)
        circ = jnp.broadcast_to(coarse_ref[j : j + 1, :], (taps, taps))
        circ = pltpu.roll(circ, 0, 1, stride=1, stride_axis=0)
        bwd_ref[at, :taps] = jnp.where(col >= row, circ, 0.0).astype(BF16)
        bwd_ref[at, taps:] = jnp.where(col < row, circ, 0.0).astype(BF16)


def table_call(coarse, turned, step):
    groups, taps = coarse.shape
    table = jax.ShapeDtypeStruct((groups * taps, 2 * taps), BF16)
    return pl.pallas_call(
        table_kernel,
        grid=(groups // step,),
        in_specs=[pl.BlockSpec((step, taps), lambda i: (i, 0))] * 2,
        out_specs=[pl.BlockSpec((step * taps, 2 * taps), lambda i: (i, 0))] * 2,
        out_shape=[table, table],
        cost_estimate=pl.CostEstimate(
            flops=groups * taps * taps * 40, bytes_accessed=groups * taps * taps * 8, transcendentals=0
        ),
        name="tables",
    )(coarse, turned)


def main_kernel(
    dot_groups,
    x_ref,
    g_ref,
    ahead_ref,
    behind_ref,
    filt_ref,
    fwd_ref,
    bwd_ref,
    out_ref,
    rim_ref,
    head_ref,
    packed_ref,
    ext,
    nxt,
    key_s,
    value_s,
    prod_s,
    grad_s,
    conv_s,
    back_s,
    lag1,
    lag2,
    fold,
):
    rows, width = x_ref.shape
    taps = ahead_ref.shape[0] - EDGE
    group_width = 16
    per = LANES // group_width
    pieces = range(0, rows, PIECE)
    ext[0:EDGE, :] = ahead_ref[taps:, :].astype(F32)
    ext[EDGE:, :] = x_ref[...].astype(F32)
    query_taps, key_taps, value_taps = (taps_of(filt_ref, i, 0, width) for i in range(3))
    nxt[0:8, :] = ext[EDGE + rows - 8 :, :]
    nxt[8:, :] = behind_ref[taps : taps + EDGE, :].astype(F32)
    query = shorten(query_taps, lambda lag: nxt[8 - lag : 8 - lag + EDGE, :])
    grad = behind_ref[taps + EDGE :, :].astype(F32) * query
    prod_s[0:taps, :] = ahead_ref[0:taps, :]
    grad_s[rows : rows + EDGE, :] = grad.astype(BF16)
    grad_s[rows + EDGE :, :] = behind_ref[EDGE:taps, :]
    for start in pieces:
        at = lambda lag: ext[EDGE + start - lag : EDGE + start - lag + PIECE, :]
        key, value = shorten(key_taps, at), shorten(value_taps, at)
        key_s[start : start + PIECE, :] = key
        value_s[start : start + PIECE, :] = value
        prod_s[taps + start : taps + start + PIECE, :] = (key * value).astype(BF16)
        grad = g_ref[start : start + PIECE, :].astype(F32) * shorten(query_taps, at)
        grad_s[start : start + PIECE, :] = grad.astype(BF16)
    lane = lax.broadcasted_iota(jnp.int32, (taps, 2 * LANES), 1) % LANES // group_width
    row = lax.broadcasted_iota(jnp.int32, (taps, taps), 0)
    col = lax.broadcasted_iota(jnp.int32, (taps, taps), 1)
    for sub in range(width // LANES):
        at = slice(sub * LANES, (sub + 1) * LANES)
        window = jnp.concatenate([prod_s[0 : 2 * taps, at], prod_s[taps : 3 * taps, at]], axis=1)
        after = jnp.concatenate([grad_s[0 : 2 * taps, at], grad_s[taps : 3 * taps, at]], axis=1)
        both = jnp.concatenate([grad_s[0:taps, at], grad_s[taps : 2 * taps, at]], axis=1)
        for table_ref, operand, result in ((fwd_ref, window, conv_s), (bwd_ref, after, back_s)):
            total = None
            for first in range(0, per, dot_groups):
                base = (sub * per + first) * taps
                part = jnp.dot(
                    table_ref[base : base + dot_groups * taps, :], operand, preferred_element_type=F32
                )
                for j in range(dot_groups):
                    mine = part[j * taps : (j + 1) * taps, :]
                    total = mine if total is None else jnp.where(lane == first + j, mine, total)
            result[0:taps, at] = total[:, :LANES]
            result[taps : 2 * taps, at] = total[:, LANES:]
        for first in range(0, per, dot_groups):
            masked = jnp.concatenate(
                [jnp.where(lane == first + j, both, jnp.zeros_like(both)) for j in range(dot_groups)], axis=0
            )
            moments = lax.dot_general(
                masked, window, (((1,), (1,)), ((), ())), preferred_element_type=F32
            )
            for j in range(dot_groups):
                mine = moments[j * taps : (j + 1) * taps, :]
                part = jnp.where(col <= row, mine[:, taps:], mine[:, :taps])
                half = taps // 2
                while half >= 8:
                    part = part[:half] + pltpu.roll(part[half:], taps - half, 1)
                    half //= 2
                fold[(first + j) * 8 : (first + j + 1) * 8, :] = part
        total = fold[pl.ds(0, per, stride=8), :]
        for r in range(1, 8):
            total = total + pltpu.roll(fold[pl.ds(r, per, stride=8), :], taps - r, 1)
        packed_ref[sub, 0:per, :] = total
    lag1[rows:, :] = jnp.zeros((8, width), F32)
    lag2[rows:, :] = jnp.zeros((8, width), F32)
    sums = [None] * 9
    by_lag = [[filt_ref[3 * i + lag : 3 * i + lag + 1, :] for i in range(3)] for lag in range(3)]
    for start in reversed(pieces):
        at = slice(start, start + PIECE)
        back = back_s[at, :]
        grads = (
            g_ref[at, :].astype(F32) * conv_s[at, :],
            back * value_s[at, :],
            back * key_s[at, :],
        )
        for lag in range(3):
            shifted = ext[EDGE + start - lag : EDGE + start - lag + PIECE, :]
            for i in range(3):
                term = grads[i] * shifted
                term = sum(term[r : r + 8] for r in range(0, PIECE, 8))
                sums[3 * i + lag] = term if sums[3 * i + lag] is None else sums[3 * i + lag] + term
        mixed = [sum(by_lag[lag][i] * grads[i] for i in range(3)) for lag in range(3)]
        lag1[at, :] = mixed[1]
        lag2[at, :] = mixed[2]
        total = mixed[0] + lag1[start + 1 : start + 1 + PIECE, :] + lag2[start + 2 : start + 2 + PIECE, :]
        out_ref[at, :] = total.astype(BF16)
        if start == rows - PIECE:
            rim_ref[...] = total[PIECE - 8 :, :]
    head_ref[0:1, :] = lag2[0:1, :]
    head_ref[1:2, :] = lag1[0:1, :] + lag2[1:2, :]
    head_ref[2:, :] = jnp.zeros((6, width), F32)
    for k in range(9):
        line = jnp.sum(sums[k], axis=0, keepdims=True)
        for sub in range(width // LANES):
            packed_ref[sub, per + k : per + k + 1, :] = line[:, sub * LANES : (sub + 1) * LANES]


def main_call(x, g, ahead, behind, filt, fwd, bwd, width, dot_groups):
    rows, chans = x.shape
    taps = ahead.shape[0] - EDGE
    groups = fwd.shape[0] // taps
    steps = chans // width
    per = groups // steps
    subs = width // LANES
    col = lambda r: pl.BlockSpec((r, width), lambda i: (0, i))
    table = pl.BlockSpec((per * taps, 2 * taps), lambda i: (i, 0))
    f32 = lambda *shape: jax.ShapeDtypeStruct(shape, F32)
    wide = lambda r, kind=F32: pltpu.VMEM((r, width), kind)
    return pl.pallas_call(
        functools.partial(main_kernel, dot_groups),
        grid=(steps,),
        in_specs=[
            col(rows), col(rows), col(taps + EDGE), col(taps + 2 * EDGE), col(filt.shape[0]), table, table,
        ],
        out_specs=[
            col(rows), col(8), col(8), pl.BlockSpec((subs, 17, taps), lambda i: (i, 0, 0)),
        ],
        out_shape=[
            jax.ShapeDtypeStruct((rows, chans), BF16), f32(8, chans), f32(8, chans),
            f32(steps * subs, 17, taps),
        ],
        scratch_shapes=[
            wide(rows + EDGE), wide(8 + EDGE), wide(rows), wide(rows), wide(rows + taps, BF16),
            wide(rows + taps, BF16), wide(rows), wide(rows), wide(rows + 8), wide(rows + 8),
            pltpu.VMEM((8 * LANES // 16, taps), F32),
        ],
        compiler_params=pltpu.CompilerParams(vmem_limit_bytes=48 * 1024 * 1024),
        cost_estimate=pl.CostEstimate(flops=26 * 10**9, bytes_accessed=24 * 2**20, transcendentals=0),
        name="operator",
    )(x, g, ahead, behind, filt, fwd, bwd)


def summed(part, inner, outer):
    inner_size, outer_size = lax.axis_size(inner), lax.axis_size(outer)
    shape = part.shape
    part = part.reshape((inner_size, shape[0] // inner_size) + shape[1:])
    part = jnp.sum(lax.all_to_all(part, inner, 0, 0, tiled=True), axis=0)
    part = lax.optimization_barrier(jnp.broadcast_to(part[None], (outer_size,) + part.shape))
    part = jnp.sum(lax.all_to_all(part, outer, 0, 0, tiled=True), axis=0)
    part = lax.optimization_barrier(jnp.broadcast_to(part[None], (inner_size,) + part.shape))
    return lax.all_to_all(part, inner, 0, 0, tiled=True).reshape(shape)


def local(inputs, short_filters, long_filter, grad_out):
    chans = inputs.shape[-1]
    rows = inputs.shape[1]
    groups, taps = long_filter.shape
    x, g = inputs[0], grad_out[0]
    filt = short_filters.reshape(9, chans)
    coarse = long_filter.astype(BF16).astype(F32)
    turned = jnp.roll(coarse[:, ::-1], 1, axis=1)
    size = lax.axis_size(SEQ)
    onward = [(i, i + 1) for i in range(size - 1)]
    back = [(i + 1, i) for i in range(size - 1)]
    ahead, behind = edge_call(x, g, filt, taps, min(512, chans))
    ahead = lax.ppermute(ahead, SEQ, onward)
    behind = lax.ppermute(behind, SEQ, back)
    fwd, bwd = table_call(coarse, turned, 16)
    out, rim, head, packed = main_call(x, g, ahead, behind, filt, fwd, bwd, min(512, chans), 2)
    head = lax.ppermute(head[:2], SEQ, back)
    rim = (rim[6:] + head).astype(BF16)
    out = lax.dynamic_update_slice(out, rim, (rows - 2, 0))
    total = inputs.shape[0] * rows * size * lax.axis_size(DP)
    packed = summed(packed, ("core", "x", "z_lo"), ("y", "z_hi")) * (1.0 / math.sqrt(total))
    per = groups // packed.shape[0]
    long = jnp.roll(packed[:, :per].reshape(groups, taps)[:, ::-1], 1, axis=1)
    short = jnp.swapaxes(packed[:, per:], 0, 1).reshape(3, 3, chans)
    return (out[None], short, long)


SEQ = ("y", "z_hi", "core")
DP = ("x", "z_lo")


def solution(mesh):
    fine = Mesh(mesh.devices.reshape(8, 4, 2, 4, 2), SEQ + DP)
    spec = P(DP, SEQ, None)
    return jax.shard_map(
        local, mesh=fine, in_specs=(spec, P(), P(), spec), out_specs=(spec, P(), P()), check_vma=False
    )
```

time: 502 us -> 108 us (0.22)
  waiting for transfers between devices: 259 us -> 17.7 us
  local copies, waits for them, and re-layouts: 150 us -> 7.67 us
  other arithmetic: 39.8 us -> 3.21 us
  Pallas kernels: 0 us -> 30 us
  starting transfers between devices: 14.7 us -> 37.1 us
  matrix products: 21.5 us -> 0 us
  between operations: 14.5 us -> 0.72 us
  blocking collectives: 0 us -> 10 us
    psum x1 -> x0, waiting for transfers between devices: 255 us -> none  [local(): grad_short, grad_long = lax.psum((grad_short, grad_long), ('seq', 'dp'))]
    reshape x7 -> x3, local copies, waits for them, and re-layouts: 42.5 us -> 2.39 us  [the longest x1 1.58 us: local(): filt = short_filters.reshape(9, chans)]
    pallas_call x0 -> x3, Pallas kernels: none -> 30 us  [the longest x1 16.8 us: main_call(): pl.pallas_call(functools.partial(main_kernel, dot_groups), grid=(steps,),...]
    another operation x6 -> x0, local copies, waits for them, and re-layouts: 26.8 us -> none  [the longest x2 17.3 us: toeplitz_tables(): jnp.tile(padded, (1, tap_count))[:, :tap_count * (period - 1)]]
    unnamed x76 -> x8, local copies, waits for them, and re-layouts: 27.2 us -> 3.36 us
    all_to_all x0 -> x2, starting transfers between devices: none -> 23.1 us  [the longest x1 16.4 us: summed(): part = jnp.sum(lax.all_to_all(part, outer, 0, 0, tiled=True), axis=0)]
    dot_general x5 -> x0, matrix products: 21.5 us -> none  [the longest x1 8.12 us: local(): jnp.einsum('snikg,snjkg->gij', grad_blocks, window, preferred_element_typ...]
    slice x18 -> x7, local copies, waits for them, and re-layouts: 15.6 us -> 0.35 us  [the longest x4 0.19 us: local(): long = jnp.roll(packed[:, :per].reshape(groups, taps)[:, ::-1], 1, axis=1)]
  transfers between devices with their start and end apart: 5 -> 5, of which waited for: 2 -> 3; matrix products, arithmetic and copies ran while one was open for 31% -> 3% of each run, Pallas kernels for 0% -> 8%
where the time goes in v1:
time: 108 us; the launch traced here: 106 us
  starting transfers between devices  37.1 us (34%)
  Pallas kernels  30 us (28%)
  waiting for transfers between devices  17.7 us (16%)
  blocking collectives  10 us (9%)
  local copies, waits for them, and re-layouts  7.67 us (7%)
  other arithmetic  3.21 us (3%)
    pallas_call x1, Pallas kernels, main_call(): pl.pallas_call(functools.partial(main_kernel, dot_groups), grid=(steps,),...  16.8 us
    all_to_all x1, starting transfers between devices, summed(): part = jnp.sum(lax.all_to_all(part, outer, 0, 0, tiled=True), axis=0)  16.4 us
    all_to_all x1, blocking collectives, summed(): part = jnp.sum(lax.all_to_all(part, inner, 0, 0, tiled=True), axis=0)  10 us
    pallas_call x1, Pallas kernels, table_call(): pl.pallas_call(table_kernel, grid=(groups // step,), in_specs=[pl.BlockSp...  9.04 us
    ppermute x1, starting transfers between devices, local(): behind = lax.ppermute(behind, SEQ, back)  8.77 us
    all_to_all x1, waiting for transfers between devices, summed(): part = jnp.sum(lax.all_to_all(part, outer, 0, 0, tiled=True), axis=0)  8.31 us
    all_to_all x1, starting transfers between devices, summed(): return lax.all_to_all(part, inner, 0, 0, tiled=True).reshape(shape)  6.7 us
    all_to_all x1, waiting for transfers between devices, summed(): return lax.all_to_all(part, inner, 0, 0, tiled=True).reshape(shape)  5.14 us
  transfers between devices with their start and end apart: 5, of which 3 were waited for; matrix products, arithmetic and copies ran while one was open for 3% of the time, Pallas kernels for 8%

profile of v1, /device:TPU:1, one launch (start us, length us, event | category | flops | bytes accessed | tf_op | source)
XLA Modules:
  0.0 106.4 jit_solution(12832775886319164356)
XLA Ops:
  0.6 1.6 %reshape.33.filt_ref = f32[9,2048]{1,0:T(8,128)} reshape(f32[3,3,2048]{2,1,0:T(4,128)} %param.5) | data formatting | bytes 147456 | tf_op jit(solution)/shard_map/reshape | solution.py:267
  2.2 4.1 %edges.1 = (bf16[144,2048]{1,0:T(8,128)(2,1)}, bf16[160,2048]{1,0:T(8,128)(2,1)}) custom-call(bf16[256,2048]{1,0:T(8,128)(2,1)} %bitcast.17, bf16[256,2048]{1,0:T(8,128)(2,1)} %bitcast.19, f32[9,2048]{1,0:T(8,128)} %reshape.33.filt_ref), custom_call_target="tpu_custom_call" | custom-call | tf_op jit(solution)/shard_map/edges/pallas_call | solution.py:49
  6.3 8.8 %collective-permute-start.1 = (bf16[160,2048]{1,0:T(8,128)(2,1)}, bf16[160,2048]{1,0:T(8,128)(2,1)S(1)}, u32[]{:S(2)}, u32[]{:S(2)}) collective-permute-start(bf16[160,2048]{1,0:T(8,128)(2,1)} %get-tuple-element.12), channel_id=1, source_target_pairs={{8,0},{16,8},{24,16},{32,24},{40,32},{48,40},{56,48},{64,56},{72,6... | collective-permute-start | bytes 1966088 | tf_op jit(solution)/shard_map/ppermute | solution.py:275
  15.1 1.9 %collective-permute-start = (bf16[144,2048]{1,0:T(8,128)(2,1)}, bf16[144,2048]{1,0:T(8,128)(2,1)S(1)}, u32[]{:S(2)}, u32[]{:S(2)}) collective-permute-start(bf16[144,2048]{1,0:T(8,128)(2,1)} %get-tuple-element.11), channel_id=1, source_target_pairs={{0,8},{8,16},{16,24},{24,32},{32,40},{40,48},{48,56},{56,64},{64,7... | collective-permute-start | bytes 1769480 | tf_op jit(solution)/shard_map/ppermute | solution.py:274
  17.1 0.8 convert_convert_fusion.coarse_ref
  17.9 0.0 copy-start.3
  17.9 0.1 slice.45
  18.0 0.1 slice.36
  18.1 0.7 pad_maximum_fusion.turned_ref
  18.8 0.0 copy-done.3
  18.8 9.0 %tables.1 = (bf16[16384,256]{1,0:T(8,128)(2,1)}, bf16[16384,256]{1,0:T(8,128)(2,1)}) custom-call(f32[128,128]{1,0:T(8,128)} %copy-done.3, f32[128,128]{1,0:T(8,128)} %pad_maximum_fusion.turned_ref), custom_call_target="tpu_custom_call" | custom-call | flops 83886080 | bytes 16777216 | tf_op jit(solution)/shard_map/tables/pallas_call | solution.py:82
  27.8 0.0 collective-permute-done.ahead_ref
  27.8 4.3 %collective-permute-done.1.behind_ref = bf16[160,2048]{1,0:T(8,128)(2,1)S(1)} collective-permute-done((bf16[160,2048]{1,0:T(8,128)(2,1)}, bf16[160,2048]{1,0:T(8,128)(2,1)S(1)}, u32[]{:S(2)}, u32[]{:S(2)}) %collective-permute-start.1) | collective-permute-done | bytes 655392 | tf_op jit(solution)/shard_map/ppermute | solution.py:275
  32.1 0.0 copy-start
  32.1 1.2 %copy-done = bf16[1,256,2048]{2,1,0:T(8,128)(2,1)S(1)} copy-done((bf16[1,256,2048]{2,1,0:T(8,128)(2,1)S(1)}, bf16[1,256,2048]{2,1,0:T(8,128)(2,1)}, u32[]{:S(2)}) %copy-start) | copy-done | bytes 1048600
  33.3 0.0 copy-start.1
  33.4 1.2 %copy-done.1 = bf16[1,256,2048]{2,1,0:T(8,128)(2,1)S(1)} copy-done((bf16[1,256,2048]{2,1,0:T(8,128)(2,1)S(1)}, bf16[1,256,2048]{2,1,0:T(8,128)(2,1)}, u32[]{:S(2)}) %copy-start.1) | copy-done | bytes 1048600
  34.6 0.0 copy-start.2
  34.6 0.9 copy-done.2
  35.5 16.8 %operator.1 = (bf16[256,2048]{1,0:T(8,128)(2,1)}, f32[8,2048]{1,0:T(8,128)S(1)}, f32[8,2048]{1,0:T(8,128)S(1)}, f32[16,17,128]{2,1,0:T(8,128)S(1)}) custom-call(bf16[256,2048]{1,0:T(8,128)(2,1)S(1)} %bitcast.18, bf16[256,2048]{1,0:T(8,128)(2,1)S(1)} %bitcast.20, bf16[144,2048]{1,0:T(8,128)(2,1)S(1)} %collective-permute-done.ahead_ref, ...), custom_call_target="tpu_custom_call" | custom-call | flops 25999998976 | bytes 25165824 | tf_op jit(solution)/shard_map/operator/pallas_call | solution.py:227
  52.3 0.1 copy.11
  52.4 10.0 %all_to_all.15 = f32[16,1,17,128]{3,1,2,0:T(1,128)S(1)} all-to-all(f32[16,1,17,128]{3,1,2,0:T(1,128)S(1)} %copy.11), channel_id=1, replica_groups=mesh['y'=8,'z_hi'=4,'core'=2,'x'=4,'z_lo'=2] {'core','x','z_lo'}, dimensions={0} | all-to-all | bytes 278528 | tf_op jit(solution)/shard_map/all_to_all | solution.py:255
  62.4 0.1 reduce_sum.18
  62.5 0.8 broadcast_in_dim.19
  63.4 16.4 %all-to-all-start.1 = ((f32[32,1,17,128]{3,1,2,0:T(1,128)}), f32[32,1,17,128]{3,1,2,0:T(1,128)S(1)}, u32[]{:S(2)}, u32[]{:S(2)}) async-start(f32[32,1,17,128]{3,1,2,0:T(1,128)} %broadcast_in_dim.19), calls=%async_computation.1 | async-start | bytes 557056 | tf_op jit(solution)/shard_map/all_to_all | solution.py:257
  79.8 3.3 %collective-permute-start.2 = (f32[2,2048]{1,0:T(2,128)S(1)}, f32[2,2048]{1,0:T(2,128)S(1)}, u32[]{:S(2)}, u32[]{:S(2)}) collective-permute-start(f32[2,2048]{1,0:T(2,128)S(1)} %slice.38), channel_id=1, source_target_pairs={{8,0},{16,8},{24,16},{32,24},{40,32},{48,40},{56,48},{64,56},{72,6... | collective-permute-start | bytes 49160 | tf_op jit(solution)/shard_map/ppermute | solution.py:278
  83.1 8.3 %all-to-all-done.1 = f32[32,1,17,128]{3,1,2,0:T(1,128)S(1)} async-done(((f32[32,1,17,128]{3,1,2,0:T(1,128)}), f32[32,1,17,128]{3,1,2,0:T(1,128)S(1)}, u32[]{:S(2)}, u32[]{:S(2)}) %all-to-all-start.1) | async-done | bytes 278560 | tf_op jit(solution)/shard_map/all_to_all | solution.py:257
  91.4 0.2 reduce_sum.19
  91.6 0.7 broadcast_in_dim.20
  92.3 6.7 %all-to-all-start.2 = ((f32[16,1,17,128]{3,1,2,0:T(1,128)}), f32[16,1,17,128]{3,1,2,0:T(1,128)S(1)}, u32[]{:S(2)}, u32[]{:S(2)}) async-start(f32[16,1,17,128]{3,1,2,0:T(1,128)} %broadcast_in_dim.20), calls=%async_computation.2 | async-start | bytes 278528 | tf_op jit(solution)/shard_map/all_to_all | solution.py:259
  99.0 0.0 collective-permute-done.2
  99.0 0.6 fusion.2
  99.6 5.1 %all-to-all-done.2 = f32[16,1,17,128]{3,1,2,0:T(1,128)S(1)} async-done(((f32[16,1,17,128]{3,1,2,0:T(1,128)}), f32[16,1,17,128]{3,1,2,0:T(1,128)S(1)}, u32[]{:S(2)}, u32[]{:S(2)}) %all-to-all-start.2) | async-done | bytes 139296 | tf_op jit(solution)/shard_map/all_to_all | solution.py:259
  104.9 0.7 reshape.35
  105.5 0.1 slice.49
  105.6 0.1 slice.43
  105.7 0.7 pad_maximum_fusion.1
  (5 shorter events, 0.1 us)
Async XLA Ops:
  6.3 25.8 %collective-permute-start.1 = (bf16[160,2048]{1,0:T(8,128)(2,1)}, bf16[160,2048]{1,0:T(8,128)(2,1)S(1)}, u32[]{:S(2)}, u32[]{:S(2)}) collective-permute-start(bf16[160,2048]{1,0:T(8,128)(2,1)} %get-tuple-element.12), channel_id=1, source_target_pairs={{8,0},{16,8},{24,16},{32,24},{40,32},{48,40},{56,48},{64,56},{72,6... | collective-permute-start | bytes 1966088 | tf_op jit(solution)/shard_map/ppermute | solution.py:275
  15.1 12.7 %collective-permute-start = (bf16[144,2048]{1,0:T(8,128)(2,1)}, bf16[144,2048]{1,0:T(8,128)(2,1)S(1)}, u32[]{:S(2)}, u32[]{:S(2)}) collective-permute-start(bf16[144,2048]{1,0:T(8,128)(2,1)} %get-tuple-element.11), channel_id=1, source_target_pairs={{0,8},{8,16},{16,24},{24,32},{32,40},{40,48},{48,56},{56,64},{64,7... | collective-permute-start | bytes 1769480 | tf_op jit(solution)/shard_map/ppermute | solution.py:274
  17.9 0.9 copy-start.3
  32.1 1.2 %copy-start = (bf16[1,256,2048]{2,1,0:T(8,128)(2,1)S(1)}, bf16[1,256,2048]{2,1,0:T(8,128)(2,1)}, u32[]{:S(2)}) copy-start(bf16[1,256,2048]{2,1,0:T(8,128)(2,1)} %param.4) | copy-start | bytes 3145732
  33.3 1.2 %copy-start.1 = (bf16[1,256,2048]{2,1,0:T(8,128)(2,1)S(1)}, bf16[1,256,2048]{2,1,0:T(8,128)(2,1)}, u32[]{:S(2)}) copy-start(bf16[1,256,2048]{2,1,0:T(8,128)(2,1)} %param.7) | copy-start | bytes 3145732
  34.6 0.9 copy-start.2
  63.4 28.1 %all-to-all-start.1 = ((f32[32,1,17,128]{3,1,2,0:T(1,128)}), f32[32,1,17,128]{3,1,2,0:T(1,128)S(1)}, u32[]{:S(2)}, u32[]{:S(2)}) async-start(f32[32,1,17,128]{3,1,2,0:T(1,128)} %broadcast_in_dim.19), calls=%async_computation.1 | async-start | bytes 557056 | tf_op jit(solution)/shard_map/all_to_all | solution.py:257
  79.8 19.2 %collective-permute-start.2 = (f32[2,2048]{1,0:T(2,128)S(1)}, f32[2,2048]{1,0:T(2,128)S(1)}, u32[]{:S(2)}, u32[]{:S(2)}) collective-permute-start(f32[2,2048]{1,0:T(2,128)S(1)} %slice.38), channel_id=1, source_target_pairs={{8,0},{16,8},{24,16},{32,24},{40,32},{48,40},{56,48},{64,56},{72,6... | collective-permute-start | bytes 49160 | tf_op jit(solution)/shard_map/ppermute | solution.py:278
  92.3 12.5 %all-to-all-start.2 = ((f32[16,1,17,128]{3,1,2,0:T(1,128)}), f32[16,1,17,128]{3,1,2,0:T(1,128)S(1)}, u32[]{:S(2)}, u32[]{:S(2)}) async-start(f32[16,1,17,128]{3,1,2,0:T(1,128)} %broadcast_in_dim.20), calls=%async_computation.2 | async-start | bytes 278528 | tf_op jit(solution)/shard_map/all_to_all | solution.py:259

commit v2 on v1

v2 whole, which is shorter than its diff:
```python
import functools
import math

import jax
import jax.numpy as jnp
from jax import lax
from jax.experimental import pallas as pl
from jax.experimental.pallas import tpu as pltpu
from jax.sharding import Mesh, PartitionSpec as P

F32 = jnp.float32
BF16 = jnp.bfloat16
LANES = 128
EDGE = 16
PIECE = 32
GROUP = 16
PER = LANES // GROUP
CHUNK = 32
VMEM_LIMIT = 12 * 1024 * 1024
UNROLL = 4
EDGE_LIMIT = 4 * 1024 * 1024
TABLE_LIMIT = 4 * 1024 * 1024


def taps_of(filt_ref, branch, lo, hi):
    return [filt_ref[branch, lag : lag + 1, lo:hi] for lag in range(3)]


def shorten(taps, rows_at):
    return taps[0] * rows_at(0) + taps[1] * rows_at(1) + taps[2] * rows_at(2)


def edge_kernel(x_ref, g_ref, filt_ref, *refs):
    (x_out, g_out, filt_out), halos, ext, sem = refs[:3], refs[3:-2], refs[-2], refs[-1]
    near_ref, far_refs = halos[0], halos[1:]
    rows = x_ref.shape[0]
    taps = ext.shape[0] - 8
    width = far_refs[0].shape[1]
    first = lax.axis_index("core") == 0
    copies = [
        pltpu.make_async_copy(source, target, sem.at[k])
        for k, (source, target) in enumerate(((filt_ref, filt_out), (x_ref, x_out), (g_ref, g_out)))
    ]
    for copy in copies:
        copy.start()
    for copy in copies:
        copy.wait()
    for part, far_ref in enumerate(far_refs):

        def tile(i, _):
            there = pl.ds(pl.multiple_of(i * LANES, LANES), LANES)
            at = pl.ds(pl.multiple_of(part * width + i * LANES, LANES), LANES)

            def give(here, ahead, behind):
                near_ref[here, at] = jnp.where(first, ahead, behind)
                far_ref[here, there] = jnp.where(first, behind, ahead)

            query_taps = [filt_out[0, lag : lag + 1, at] for lag in range(3)]
            ext[0:8, :] = jnp.zeros((8, LANES), F32)
            ext[8:, :] = x_out[0:taps, at].astype(F32)
            for start in range(0, taps, PIECE):
                here = slice(start, start + PIECE)
                query = shorten(query_taps, lambda lag: ext[8 + start - lag : 8 + start - lag + PIECE, :])
                tail = rows - taps - EDGE + start
                give(
                    here,
                    x_out[tail : tail + PIECE, at],
                    (g_out[here, at].astype(F32) * query).astype(BF16),
                )
            rim = jnp.concatenate([ext[8:16, :], g_out[0:EDGE, at].astype(F32)[0:8]], axis=0)
            give(slice(taps, taps + EDGE), x_out[rows - EDGE :, at], rim.astype(BF16))
            return 0

        lax.fori_loop(0, width // LANES, tile, 0)


def edge_call(x, g, filters, taps, parts):
    chans = x.shape[1]
    halo = lambda width: jax.ShapeDtypeStruct((taps + EDGE, width), BF16)
    same = [jax.ShapeDtypeStruct(a.shape, a.dtype) for a in (x, g, filters)]
    made = pl.pallas_call(
        edge_kernel,
        in_specs=[pl.BlockSpec(memory_space=pltpu.HBM)] * 3,
        out_specs=[pl.BlockSpec(memory_space=pltpu.VMEM)] * (4 + parts),
        out_shape=same + [halo(chans)] + [halo(chans // parts)] * parts,
        scratch_shapes=[pltpu.VMEM((taps + 8, LANES), F32), pltpu.SemaphoreType.DMA((3,))],
        compiler_params=pltpu.CompilerParams(vmem_limit_bytes=EDGE_LIMIT),
        name="edges",
    )(x, g, filters)
    return made[:3], made[3], made[4:]


def table_kernel(filter_ref, fwd_ref, bwd_ref):
    taps = filter_ref.shape[1]
    row = lax.broadcasted_iota(jnp.int32, (taps, taps), 0)
    col = lax.broadcasted_iota(jnp.int32, (taps, taps), 1)
    lead = lax.broadcasted_iota(jnp.int32, (8, taps), 1)
    zero = jnp.zeros((taps, taps), BF16)
    chunks = taps // CHUNK

    def tile(sub, _):
        coarse = filter_ref[pl.ds(pl.multiple_of(sub * PER, PER), PER), :].astype(BF16).astype(F32)
        turned = jnp.take_along_axis(coarse, (taps - lead) % taps, axis=1)
        for j in range(PER):
            for out_ref, source, early, late in (
                (fwd_ref, turned, col > row, col <= row),
                (bwd_ref, coarse, col >= row, col < row),
            ):
                circ = jnp.broadcast_to(source[j : j + 1, :], (taps, taps))
                circ = pltpu.roll(circ, 0, 1, stride=1, stride_axis=0).astype(BF16)
                early, late = jnp.where(early, circ, zero), jnp.where(late, circ, zero)
                for r in range(chunks):
                    base = ((sub * chunks + r) * PER + j) * CHUNK
                    rows = pl.ds(pl.multiple_of(base, CHUNK), CHUNK)
                    here = slice(r * CHUNK, (r + 1) * CHUNK)
                    out_ref[rows, :taps] = early[here]
                    out_ref[rows, taps:] = late[here]
        return 0

    lax.fori_loop(0, filter_ref.shape[0] // PER, tile, 0, unroll=UNROLL)


def table_call(long_filter):
    groups, taps = long_filter.shape
    table = jax.ShapeDtypeStruct((groups * taps, 2 * taps), BF16)
    return pl.pallas_call(
        table_kernel,
        in_specs=[pl.BlockSpec(memory_space=pltpu.VMEM)],
        out_specs=[pl.BlockSpec(memory_space=pltpu.VMEM)] * 2,
        out_shape=[table, table],
        cost_estimate=pl.CostEstimate(
            flops=groups * taps * taps * 40, bytes_accessed=groups * taps * taps * 8, transcendentals=0
        ),
        compiler_params=pltpu.CompilerParams(vmem_limit_bytes=TABLE_LIMIT),
        name="tables",
    )(long_filter)


def main_kernel(
    cfg,
    scale,
    x_ref,
    g_ref,
    near_ref,
    far_ref,
    filt_ref,
    fwd_ref,
    bwd_ref,
    out_ref,
    rim_ref,
    head_ref,
    packed_ref,
    ext,
    key_s,
    value_s,
    prod_s,
    grad_s,
    lag0,
    lag1,
    lag2,
    fold,
):
    rows, width = x_ref.shape[0], cfg[0]
    taps = far_ref.shape[0] - EDGE
    lead = far_ref.shape[0]
    first = lax.axis_index("core") == 0
    chunks = taps // CHUNK
    subs = width // LANES
    lane = lax.broadcasted_iota(jnp.int32, (CHUNK, 2 * LANES), 1) % LANES // GROUP
    lane_all = lax.broadcasted_iota(jnp.int32, (taps, 2 * LANES), 1) % LANES // GROUP
    row = lax.broadcasted_iota(jnp.int32, (taps, taps), 0)
    col = lax.broadcasted_iota(jnp.int32, (taps, taps), 1)
    below = col <= row
    head_ref[2:, :] = jnp.zeros((6, head_ref.shape[1]), F32)

    chans = out_ref.shape[1]
    skip = cfg[1] * chans

    def lanes_of(tile):
        at = pl.multiple_of(tile * LANES, LANES)
        return pl.ds(at, LANES), pl.ds(pl.multiple_of(skip + at, LANES), LANES)

    def filters(at):
        return [[filt_ref[i, lag : lag + 1, at] for lag in range(3)] for i in range(3)]

    def gates(tile, sub):
        at, of = lanes_of(tile)
        query_taps, key_taps, value_taps = filters(of)
        near, far = near_ref[:, of], far_ref[:, at]
        ahead, behind = jnp.where(first, far, near), jnp.where(first, near, far)
        ext[sub, 0:lead, :] = ahead.astype(F32)
        ext[sub, lead : lead + rows, :] = x_ref[:, of].astype(F32)
        rim = behind[taps:].astype(F32)
        ext[sub, lead + rows :, :] = rim[0:8]
        query = shorten(
            query_taps, lambda lag: ext[sub, lead + rows - lag : lead + rows - lag + 8, :]
        )
        head = jnp.concatenate([(rim[8:] * query)[0:2], behind[0:EDGE].astype(F32)[2:]], axis=0)
        grad_s[sub, rows : rows + EDGE, :] = head.astype(BF16)
        grad_s[sub, rows + EDGE :, :] = behind[EDGE:taps]
        yield
        for start in range(-taps, rows, PIECE):
            base = lead + start
            lagged = [ext[sub, base - lag : base - lag + PIECE, :] for lag in range(3)]
            key, value = (shorten(t, lambda lag: lagged[lag]) for t in (key_taps, value_taps))
            prod_s[sub, taps + start : taps + start + PIECE, :] = (key * value).astype(BF16)
            if start >= 0:
                here = slice(start, start + PIECE)
                key_s[sub, here, :] = key
                value_s[sub, here, :] = value
                query = shorten(query_taps, lambda lag: lagged[lag])
                grad_s[sub, here, :] = (g_ref[here, of].astype(F32) * query).astype(BF16)
            yield

    def work(tile, sub):
        at, of = lanes_of(tile)
        taken = filters(of)
        window = jnp.concatenate([prod_s[sub, 0 : 2 * taps, :], prod_s[sub, taps:, :]], axis=1)
        after = jnp.concatenate([grad_s[sub, 0 : 2 * taps, :], grad_s[sub, taps:, :]], axis=1)
        both = jnp.concatenate([grad_s[sub, 0:taps, :], grad_s[sub, taps : 2 * taps, :]], axis=1)
        sums = [jnp.zeros((8, LANES), F32) for _ in range(9)]
        span = PER * CHUNK

        def picked(table_ref, operand, r):
            base = pl.multiple_of(((skip // LANES + tile) * chunks + r) * span, span)
            part = jnp.dot(table_ref[pl.ds(base, span), :], operand, preferred_element_type=F32)
            total = part[0:CHUNK]
            for j in range(1, PER):
                total = jnp.where(lane == j, part[j * CHUNK : (j + 1) * CHUNK], total)
            return total

        each = PER // chunks
        for r in range(chunks):
            conv, back = picked(fwd_ref, window, r), picked(bwd_ref, after, r)
            yield
            for block in range(2):
                here = slice(block * taps + r * CHUNK, block * taps + (r + 1) * CHUNK)
                wide = slice(block * LANES, (block + 1) * LANES)
                grads = (
                    g_ref[here, of].astype(F32) * conv[:, wide],
                    back[:, wide] * value_s[sub, here, :],
                    back[:, wide] * key_s[sub, here, :],
                )
                for lag in range(3):
                    base = lead + here.start - lag
                    shifted = ext[sub, base : base + CHUNK, :]
                    for i in range(3):
                        term = grads[i] * shifted
                        sums[3 * i + lag] += sum(term[k : k + 8] for k in range(0, CHUNK, 8))
                for lag, keep in enumerate((lag0, lag1, lag2)):
                    keep[sub, here, :] = sum(taken[i][lag] * grads[i] for i in range(3))
                yield
            masked = jnp.concatenate(
                [
                    jnp.where(lane_all == r * each + j, both, jnp.zeros_like(both))
                    for j in range(each)
                ],
                axis=0,
            )
            moments = lax.dot_general(
                masked, window, (((1,), (1,)), ((), ())), preferred_element_type=F32
            )
            for j in range(each):
                mine = moments[j * taps : (j + 1) * taps, :]
                part = jnp.where(below, mine[:, taps:], mine[:, :taps])
                half = taps // 2
                while half >= 8:
                    part = part[:half] + pltpu.roll(part[half:], taps - half, 1)
                    half //= 2
                slot = (r * each + j) * 8
                fold[sub, slot : slot + 8, :] = part
            yield
        for k in range(9):
            line = jnp.sum(sums[k], axis=0, keepdims=True) * scale
            packed_ref[tile, PER + k : PER + k + 1, :] = line

    def finish(tile, sub):
        at, of = lanes_of(tile)
        total = fold[sub, pl.ds(0, PER, stride=8), :]
        for r in range(1, 8):
            total = total + pltpu.roll(fold[sub, pl.ds(r, PER, stride=8), :], taps - r, 1)
        turn = (taps - lax.broadcasted_iota(jnp.int32, (PER, taps), 1)) % taps
        packed_ref[tile, 0:PER, :] = jnp.take_along_axis(total, turn, axis=1) * scale
        lag1[sub, rows:, :] = jnp.zeros((8, LANES), F32)
        lag2[sub, rows:, :] = jnp.zeros((8, LANES), F32)
        yield
        for start in range(0, rows, PIECE):
            here = slice(start, start + PIECE)
            total = (
                lag0[sub, here, :]
                + lag1[sub, start + 1 : start + 1 + PIECE, :]
                + lag2[sub, start + 2 : start + 2 + PIECE, :]
            )
            out_ref[here, at] = total.astype(BF16)
            if start == rows - PIECE:
                rim_ref[:, at] = total[PIECE - 8 :, :]
            yield
        head_ref[0:1, at] = lag2[sub, 0:1, :]
        head_ref[1:2, at] = lag1[sub, 0:1, :] + lag2[sub, 1:2, :]

    tiles = chans // LANES

    def drain(*others):
        for other in others:
            for _ in other:
                pass

    def turn(step, _):
        for sub in range(subs):
            tile = step * subs + sub
            beside = (
                gates(jnp.minimum(tile + 1, tiles - 1), (sub + 1) % subs),
                finish(jnp.maximum(tile - 1, 0), (sub - 1) % subs),
            )
            for _ in work(tile, sub):
                for other in beside:
                    next(other, None)
            drain(*beside)
        return 0

    drain(gates(0, 0))
    lax.fori_loop(0, tiles // subs, turn, 0)
    drain(finish(tiles - 1, subs - 1))


def main_call(x, g, near, far, filters, fwd, bwd, width, scale, part):
    rows, chans = x.shape[0], far.shape[1]
    lead, taps = far.shape[0], far.shape[0] - EDGE
    width = min(width, chans)
    subs = width // LANES
    f32 = lambda *shape: jax.ShapeDtypeStruct(shape, F32)
    wide = lambda r, kind=F32: pltpu.VMEM((subs, r, LANES), kind)
    return pl.pallas_call(
        functools.partial(main_kernel, (width, part, CHUNK, PIECE), scale),
        in_specs=[pl.BlockSpec(memory_space=pltpu.VMEM)] * 7,
        out_specs=[pl.BlockSpec(memory_space=pltpu.VMEM)] * 4,
        out_shape=[
            jax.ShapeDtypeStruct((rows, chans), BF16), f32(8, chans), f32(8, chans),
            f32(chans // LANES, PER + 9, taps),
        ],
        scratch_shapes=[
            wide(lead + rows + 8), wide(rows), wide(rows), wide(rows + taps, BF16),
            wide(rows + taps, BF16), wide(rows), wide(rows + 8), wide(rows + 8), wide(8 * PER),
        ],
        compiler_params=pltpu.CompilerParams(vmem_limit_bytes=VMEM_LIMIT),
        cost_estimate=pl.CostEstimate(flops=26 * 10**9, bytes_accessed=24 * 2**20, transcendentals=0),
        name="operator",
    )(x, g, near, far, filters, fwd, bwd)


def unpack_kernel(part_ref, short_ref, long_ref):
    rows = PER + 9
    for tile in range(part_ref.shape[0] // rows):
        base = tile * rows
        long_ref[tile * PER : (tile + 1) * PER, :] = part_ref[base : base + PER, :]
        for k in range(9):
            at = base + PER + k
            short_ref[k // 3, k % 3 : k % 3 + 1, tile * LANES : (tile + 1) * LANES] = part_ref[at : at + 1, :]


def on_vmem(kernel, name, out, *operands):
    return pl.pallas_call(
        kernel,
        in_specs=[pl.BlockSpec(memory_space=pltpu.VMEM)] * len(operands),
        out_specs=jax.tree.map(lambda _: pl.BlockSpec(memory_space=pltpu.VMEM), out),
        out_shape=out,
        compiler_params=pltpu.CompilerParams(vmem_limit_bytes=TABLE_LIMIT),
        name=name,
    )(*operands)


def summed(part, inner, outer):
    inner_size, outer_size = lax.axis_size(inner), lax.axis_size(outer)
    shape = part.shape
    part = part.reshape((inner_size, shape[0] // inner_size) + shape[1:])
    part = jnp.sum(lax.all_to_all(part, inner, 0, 0, tiled=True), axis=0)
    part = lax.optimization_barrier(jnp.broadcast_to(part[None], (outer_size,) + part.shape))
    part = jnp.sum(lax.all_to_all(part, outer, 0, 0, tiled=True), axis=0)
    part = lax.optimization_barrier(jnp.broadcast_to(part[None], (inner_size,) + part.shape))
    return lax.all_to_all(part, inner, 0, 0, tiled=True).reshape(shape)


PARTS = 2
WIDTH = 1024


def local(inputs, short_filters, long_filter, grad_out):
    chans = inputs.shape[-1]
    rows = inputs.shape[1]
    groups, taps = long_filter.shape
    x, g = inputs[0], grad_out[0]
    size = lax.axis_size(SEQ)
    within = [(i, i ^ 1) for i in range(size)]
    between = [(i, i + 1) for i in range(1, size - 1, 2)] + [(i + 1, i) for i in range(1, size - 1, 2)]
    back = [(i + 1, i) for i in range(size - 1)]
    total = inputs.shape[0] * rows * size * lax.axis_size(DP)
    scale = 1.0 / math.sqrt(total)
    (x, g, filters), near, far = edge_call(x, g, short_filters, taps, PARTS)
    near = lax.ppermute(near, SEQ, within)
    far = [lax.ppermute(rows_of, SEQ, between) for rows_of in far]
    fwd, bwd = table_call(long_filter)
    done = [
        main_call(x, g, near, far[k], filters, fwd, bwd, WIDTH, scale, k)
        for k in range(PARTS)
    ]
    out, rim, head, packed = (
        jnp.concatenate([d[i] for d in done], axis=(1, 1, 1, 0)[i]) for i in range(4)
    )
    head = lax.ppermute(head[:2], SEQ, back)
    rim = (rim[6:] + head).astype(BF16)
    out = lax.dynamic_update_slice(out, rim, (rows - 2, 0))
    packed = summed(packed, ("core", "x", "z_lo"), ("y", "z_hi"))
    short, long = on_vmem(
        unpack_kernel,
        "unpack",
        (jax.ShapeDtypeStruct((3, 3, chans), F32), jax.ShapeDtypeStruct((groups, taps), F32)),
        packed.reshape(-1, taps),
    )
    return (out[None], short, long)


SEQ = ("y", "z_hi", "core")
DP = ("x", "z_lo")
DIMS = (8, 4, 2, 4, 2)


def solution(mesh):
    fine = Mesh(mesh.devices.reshape(DIMS), SEQ + DP)
    spec = P(DP, SEQ, None)
    return jax.shard_map(
        local, mesh=fine, in_specs=(spec, P(), P(), spec), out_specs=(spec, P(), P()), check_vma=False
    )
```

time: 108 us -> 90.8 us (0.84)
  Pallas kernels: 30 us -> 17.9 us
  starting transfers between devices: 37.1 us -> 40.4 us
  other arithmetic: 3.21 us -> 0.4 us
  local copies, waits for them, and re-layouts: 7.67 us -> 5.07 us
  blocking collectives: 10 us -> 7.96 us
    pallas_call x3 -> x5, Pallas kernels: 30 us -> 17.9 us  [the longest x2 12.4 us: main_call(): pl.pallas_call(functools.partial(main_kernel, (width, part, CHUNK, PIECE)...]
    ppermute x2 -> x3, starting transfers between devices: 10.7 us -> 15.2 us  [the longest x1 8.79 us: local(): near = lax.ppermute(near, SEQ, within)]
    reshape x2 -> x0, local copies, waits for them, and re-layouts: 2.25 us -> none  [the longest x1 1.58 us: local(): filt = short_filters.reshape(9, chans)]
    all_to_all x1, blocking collectives: 10 us -> 7.96 us  [summed(): part = jnp.sum(lax.all_to_all(part, inner, 0, 0, tiled=True), axis=0)]
    concatenate x2 -> x1, other arithmetic: 1.47 us -> 0.01 us  [local(): jnp.concatenate([d[i] for d in done], axis=(1, 1, 1, 0)[i])]
    all_to_all x1, starting transfers between devices: 16.4 us -> 15.2 us  [summed(): part = jnp.sum(lax.all_to_all(part, outer, 0, 0, tiled=True), axis=0)]
    ppermute x2 -> x3, waiting for transfers between devices: 4.28 us -> 3.1 us  [the longest x2 3.09 us: local(): far = [lax.ppermute(rows_of, SEQ, between) for rows_of in far]]
    unnamed x8 -> x10, local copies, waits for them, and re-layouts: 3.36 us -> 3.34 us
  transfers between devices with their start and end apart: 5 -> 6, of which waited for: 3 -> 4; matrix products, arithmetic and copies ran while one was open for 3% -> 1% of each run, Pallas kernels for 8% -> 11%
where the time goes in v2:
time: 90.8 us; the launch traced here: 89.6 us
  starting transfers between devices  40.4 us (44%)
  Pallas kernels  17.9 us (20%)
  waiting for transfers between devices  17 us (19%)
  blocking collectives  7.96 us (9%)
  local copies, waits for them, and re-layouts  5.07 us (6%)
    all_to_all x1, starting transfers between devices, summed(): part = jnp.sum(lax.all_to_all(part, outer, 0, 0, tiled=True), axis=0)  15.2 us
    pallas_call x2, Pallas kernels, main_call(): pl.pallas_call(functools.partial(main_kernel, (width, part, CHUNK, PIECE)...  12.4 us
    ppermute x1, starting transfers between devices, local(): near = lax.ppermute(near, SEQ, within)  8.79 us
    all_to_all x1, waiting for transfers between devices, summed(): part = jnp.sum(lax.all_to_all(part, outer, 0, 0, tiled=True), axis=0)  8.22 us
    all_to_all x1, blocking collectives, summed(): part = jnp.sum(lax.all_to_all(part, inner, 0, 0, tiled=True), axis=0)  7.96 us
    all_to_all x1, starting transfers between devices, summed(): return lax.all_to_all(part, inner, 0, 0, tiled=True).reshape(shape)  6.7 us
    ppermute x2, starting transfers between devices, local(): far = [lax.ppermute(rows_of, SEQ, between) for rows_of in far]  6.46 us
    all_to_all x1, waiting for transfers between devices, summed(): return lax.all_to_all(part, inner, 0, 0, tiled=True).reshape(shape)  5.71 us
  transfers between devices with their start and end apart: 6, of which 4 were waited for; matrix products, arithmetic and copies ran while one was open for 1% of the time, Pallas kernels for 11%

profile of v2, /device:TPU:1, one launch (start us, length us, event | category | flops | bytes accessed | tf_op | source)
XLA Modules:
  0.0 89.6 jit_solution(6991764514656020655)
XLA Ops:
  0.6 0.0 copy-start
  0.6 1.2 %copy-done = bf16[1,256,2048]{2,1,0:T(8,128)(2,1)S(1)} copy-done((bf16[1,256,2048]{2,1,0:T(8,128)(2,1)S(1)}, bf16[1,256,2048]{2,1,0:T(8,128)(2,1)}, u32[]{:S(2)}) %copy-start) | copy-done | bytes 1048600
  1.9 0.0 copy-start.1
  1.9 1.2 %copy-done.1 = bf16[1,256,2048]{2,1,0:T(8,128)(2,1)S(1)} copy-done((bf16[1,256,2048]{2,1,0:T(8,128)(2,1)S(1)}, bf16[1,256,2048]{2,1,0:T(8,128)(2,1)}, u32[]{:S(2)}) %copy-start.1) | copy-done | bytes 1048600
  3.1 0.0 copy-start.2
  3.1 0.9 copy-done.2
  4.0 0.0 copy-start.3
  4.0 1.1 %edges.1 = (bf16[256,2048]{1,0:T(8,128)(2,1)S(1)}, bf16[256,2048]{1,0:T(8,128)(2,1)S(1)}, f32[3,3,2048]{2,1,0:T(4,128)S(1)}, bf16[144,2048]{1,0:T(8,128)(2,1)S(1...) custom-call(bf16[256,2048]{1,0:T(8,128)(2,1)S(1)} %bitcast.9, bf16[256,2048]{1,0:T(8,128)(2,1)S(1)} %bitcast.10, ...), custom_call_target="tpu_custom_call" | custom-call | tf_op jit(solution)/shard_map/edges/pallas_call | solution.py:81
  5.1 8.8 %collective-permute-start = (bf16[144,2048]{1,0:T(8,128)(2,1)S(1)}, bf16[144,2048]{1,0:T(8,128)(2,1)S(1)}, u32[]{:S(2)}, u32[]{:S(2)}) collective-permute-start(bf16[144,2048]{1,0:T(8,128)(2,1)S(1)} %get-tuple-element.23), channel_id=1, source_target_pairs={{0,8},{8,0},{16,24},{24,16},{32,40},{40,32},{48,56},{56,48},{64,72... | collective-permute-start | bytes 1769480 | tf_op jit(solution)/shard_map/ppermute | solution.py:399
  13.9 1.9 %collective-permute-start.2 = (bf16[144,1024]{1,0:T(8,128)(2,1)S(1)}, bf16[144,1024]{1,0:T(8,128)(2,1)S(1)}, u32[]{:S(2)}, u32[]{:S(2)}) collective-permute-start(bf16[144,1024]{1,0:T(8,128)(2,1)S(1)} %get-tuple-element.29), channel_id=1, source_target_pairs={{8,16},{24,32},{40,48},{56,64},{72,80},{88,96},{104,112},{120,128}... | collective-permute-start | bytes 884744 | tf_op jit(solution)/shard_map/ppermute | solution.py:400
  15.8 4.5 %collective-permute-start.1 = (bf16[144,1024]{1,0:T(8,128)(2,1)S(1)}, bf16[144,1024]{1,0:T(8,128)(2,1)S(1)}, u32[]{:S(2)}, u32[]{:S(2)}) collective-permute-start(bf16[144,1024]{1,0:T(8,128)(2,1)S(1)} %get-tuple-element.24), channel_id=1, source_target_pairs={{8,16},{24,32},{40,48},{56,64},{72,80},{88,96},{104,112},{120,128}... | collective-permute-start | bytes 884744 | tf_op jit(solution)/shard_map/ppermute | solution.py:400
  20.3 0.0 copy-done.3
  20.3 3.7 %tables.1 = (bf16[16384,256]{1,0:T(8,128)(2,1)S(1)}, bf16[16384,256]{1,0:T(8,128)(2,1)S(1)}) custom-call(f32[128,128]{1,0:T(8,128)S(1)} %copy-done.3), custom_call_target="tpu_custom_call" | custom-call | flops 83886080 | bytes 16777216 | tf_op jit(solution)/shard_map/tables/pallas_call | solution.py:126
  24.1 2.9 %collective-permute-done.2.far_ref = bf16[144,1024]{1,0:T(8,128)(2,1)S(1)} collective-permute-done((bf16[144,1024]{1,0:T(8,128)(2,1)S(1)}, bf16[144,1024]{1,0:T(8,128)(2,1)S(1)}, u32[]{:S(2)}, u32[]{:S(2)}) %collective-permute-start.2) | collective-permute-done | bytes 294944 | tf_op jit(solution)/shard_map/ppermute | solution.py:400
  27.0 0.0 collective-permute-done.near_ref
  27.0 6.2 %operator.3 = (bf16[256,1024]{1,0:T(8,128)(2,1)S(1)}, f32[8,1024]{1,0:T(8,128)S(1)}, f32[8,1024]{1,0:T(8,128)S(1)}, f32[8,17,128]{2,1,0:T(8,128)S(1)}) custom-call(bf16[256,2048]{1,0:T(8,128)(2,1)S(1)} %get-tuple-element.21.x_ref, bf16[256,2048]{1,0:T(8,128)(2,1)S(1)} %get-tuple-element.22.g_ref, bf16[144,2048]{1,0:T(8,128)(2,1)S(1)} %collective-permute-done.near_ref, ...), custom_call_target="tpu_custom_call" | custom-call | flops 25999998976 | bytes 25165824 | tf_op jit(solution)/shard_map/operator/pallas_call | solution.py:333
  33.2 0.2 collective-permute-done.1.far_ref
  33.4 6.2 %operator.2 = (bf16[256,1024]{1,0:T(8,128)(2,1)S(1)}, f32[8,1024]{1,0:T(8,128)S(1)}, f32[8,1024]{1,0:T(8,128)S(1)}, f32[8,17,128]{2,1,0:T(8,128)S(1)}) custom-call(bf16[256,2048]{1,0:T(8,128)(2,1)S(1)} %get-tuple-element.21.x_ref, bf16[256,2048]{1,0:T(8,128)(2,1)S(1)} %get-tuple-element.22.g_ref, bf16[144,2048]{1,0:T(8,128)(2,1)S(1)} %collective-permute-done.near_ref, ...), custom_call_target="tpu_custom_call" | custom-call | flops 25999998976 | bytes 25165824 | tf_op jit(solution)/shard_map/operator/pallas_call | solution.py:333
  39.6 0.1 copy.7
  39.8 8.0 %all_to_all.15 = f32[16,1,17,128]{3,1,2,0:T(1,128)S(1)} all-to-all(f32[16,1,17,128]{3,1,2,0:T(1,128)S(1)} %copy.7), channel_id=1, replica_groups=mesh['y'=8,'z_hi'=4,'core'=2,'x'=4,'z_lo'=2] {'core','x','z_lo'}, dimensions={0} | all-to-all | bytes 278528 | tf_op jit(solution)/shard_map/all_to_all | solution.py:376
  47.7 0.1 reduce_sum.18
  47.8 0.9 broadcast_in_dim.19
  48.7 15.2 %all-to-all-start.1 = ((f32[32,1,17,128]{3,1,2,0:T(1,128)}), f32[32,1,17,128]{3,1,2,0:T(1,128)S(1)}, u32[]{:S(2)}, u32[]{:S(2)}) async-start(f32[32,1,17,128]{3,1,2,0:T(1,128)} %broadcast_in_dim.19), calls=%async_computation.1 | async-start | bytes 557056 | tf_op jit(solution)/shard_map/all_to_all | solution.py:378
  63.9 3.3 %collective-permute-start.3 = (f32[2,2048]{1,0:T(2,128)S(1)}, f32[2,2048]{1,0:T(2,128)S(1)}, u32[]{:S(2)}, u32[]{:S(2)}) collective-permute-start(f32[2,2048]{1,0:T(2,128)S(1)} %pad_maximum_fusion), channel_id=1, source_target_pairs={{8,0},{16,8},{24,16},{32,24},{40,32},{48,40},{56,48},{64,56},{72,6... | collective-permute-start | bytes 49160 | tf_op jit(solution)/shard_map/ppermute | solution.py:409
  67.2 0.1 maximum_bitcast_fusion
  67.3 8.2 %all-to-all-done.1 = f32[32,1,17,128]{3,1,2,0:T(1,128)S(1)} async-done(((f32[32,1,17,128]{3,1,2,0:T(1,128)}), f32[32,1,17,128]{3,1,2,0:T(1,128)S(1)}, u32[]{:S(2)}, u32[]{:S(2)}) %all-to-all-start.1) | async-done | bytes 278560 | tf_op jit(solution)/shard_map/all_to_all | solution.py:378
  75.5 0.2 reduce_sum.19
  75.7 0.7 broadcast_in_dim.20
  76.4 6.7 %all-to-all-start.2 = ((f32[16,1,17,128]{3,1,2,0:T(1,128)}), f32[16,1,17,128]{3,1,2,0:T(1,128)S(1)}, u32[]{:S(2)}, u32[]{:S(2)}) async-start(f32[16,1,17,128]{3,1,2,0:T(1,128)} %broadcast_in_dim.20), calls=%async_computation.2 | async-start | bytes 278528 | tf_op jit(solution)/shard_map/all_to_all | solution.py:380
  83.1 0.0 collective-permute-done.3
  83.2 0.0 copy-start.4
  83.2 5.7 %all-to-all-done.2 = f32[16,1,17,128]{3,1,2,0:T(1,128)S(1)} async-done(((f32[16,1,17,128]{3,1,2,0:T(1,128)}), f32[16,1,17,128]{3,1,2,0:T(1,128)S(1)}, u32[]{:S(2)}, u32[]{:S(2)}) %all-to-all-start.2) | async-done | bytes 139296 | tf_op jit(solution)/shard_map/all_to_all | solution.py:380
  88.9 0.7 unpack.1
  89.6 0.0 copy-done.4
  (3 shorter events, 0.1 us)
Async XLA Ops:
  0.6 1.2 %copy-start = (bf16[1,256,2048]{2,1,0:T(8,128)(2,1)S(1)}, bf16[1,256,2048]{2,1,0:T(8,128)(2,1)}, u32[]{:S(2)}) copy-start(bf16[1,256,2048]{2,1,0:T(8,128)(2,1)} %param.4) | copy-start | bytes 3145732
  1.9 1.2 %copy-start.1 = (bf16[1,256,2048]{2,1,0:T(8,128)(2,1)S(1)}, bf16[1,256,2048]{2,1,0:T(8,128)(2,1)}, u32[]{:S(2)}) copy-start(bf16[1,256,2048]{2,1,0:T(8,128)(2,1)} %param.7) | copy-start | bytes 3145732
  3.1 0.9 copy-start.2
  4.0 16.4 %copy-start.3 = (f32[128,128]{1,0:T(8,128)S(1)}, f32[128,128]{1,0:T(8,128)}, u32[]{:S(2)}) copy-start(f32[128,128]{1,0:T(8,128)} %filter_ref.1) | copy-start | bytes 196612
  5.1 22.0 %collective-permute-start = (bf16[144,2048]{1,0:T(8,128)(2,1)S(1)}, bf16[144,2048]{1,0:T(8,128)(2,1)S(1)}, u32[]{:S(2)}, u32[]{:S(2)}) collective-permute-start(bf16[144,2048]{1,0:T(8,128)(2,1)S(1)} %get-tuple-element.23), channel_id=1, source_target_pairs={{0,8},{8,0},{16,24},{24,16},{32,40},{40,32},{48,56},{56,48},{64,72... | collective-permute-start | bytes 1769480 | tf_op jit(solution)/shard_map/ppermute | solution.py:399
  13.9 13.2 %collective-permute-start.2 = (bf16[144,1024]{1,0:T(8,128)(2,1)S(1)}, bf16[144,1024]{1,0:T(8,128)(2,1)S(1)}, u32[]{:S(2)}, u32[]{:S(2)}) collective-permute-start(bf16[144,1024]{1,0:T(8,128)(2,1)S(1)} %get-tuple-element.29), channel_id=1, source_target_pairs={{8,16},{24,32},{40,48},{56,64},{72,80},{88,96},{104,112},{120,128}... | collective-permute-start | bytes 884744 | tf_op jit(solution)/shard_map/ppermute | solution.py:400
  15.8 17.6 %collective-permute-start.1 = (bf16[144,1024]{1,0:T(8,128)(2,1)S(1)}, bf16[144,1024]{1,0:T(8,128)(2,1)S(1)}, u32[]{:S(2)}, u32[]{:S(2)}) collective-permute-start(bf16[144,1024]{1,0:T(8,128)(2,1)S(1)} %get-tuple-element.24), channel_id=1, source_target_pairs={{8,16},{24,32},{40,48},{56,64},{72,80},{88,96},{104,112},{120,128}... | collective-permute-start | bytes 884744 | tf_op jit(solution)/shard_map/ppermute | solution.py:400
  48.7 26.8 %all-to-all-start.1 = ((f32[32,1,17,128]{3,1,2,0:T(1,128)}), f32[32,1,17,128]{3,1,2,0:T(1,128)S(1)}, u32[]{:S(2)}, u32[]{:S(2)}) async-start(f32[32,1,17,128]{3,1,2,0:T(1,128)} %broadcast_in_dim.19), calls=%async_computation.1 | async-start | bytes 557056 | tf_op jit(solution)/shard_map/all_to_all | solution.py:378
  63.9 19.2 %collective-permute-start.3 = (f32[2,2048]{1,0:T(2,128)S(1)}, f32[2,2048]{1,0:T(2,128)S(1)}, u32[]{:S(2)}, u32[]{:S(2)}) collective-permute-start(f32[2,2048]{1,0:T(2,128)S(1)} %pad_maximum_fusion), channel_id=1, source_target_pairs={{8,0},{16,8},{24,16},{32,24},{40,32},{48,40},{56,48},{64,56},{72,6... | collective-permute-start | bytes 49160 | tf_op jit(solution)/shard_map/ppermute | solution.py:409
  76.4 12.5 %all-to-all-start.2 = ((f32[16,1,17,128]{3,1,2,0:T(1,128)}), f32[16,1,17,128]{3,1,2,0:T(1,128)S(1)}, u32[]{:S(2)}, u32[]{:S(2)}) async-start(f32[16,1,17,128]{3,1,2,0:T(1,128)} %broadcast_in_dim.20), calls=%async_computation.2 | async-start | bytes 278528 | tf_op jit(solution)/shard_map/all_to_all | solution.py:380
  83.2 6.4 %copy-start.4 = (bf16[1,256,2048]{2,1,0:T(8,128)(2,1)}, bf16[1,256,2048]{2,1,0:T(8,128)(2,1)S(1)}, u32[]{:S(2)}) copy-start(bf16[1,256,2048]{2,1,0:T(8,128)(2,1)S(1)} %bitcast_dynamic-update-slice_fusion) | copy-start | bytes 3145732

commit v3 on v2

--- a/solution.py
+++ b/solution.py
@@ -39,11 +39,18 @@
     first = lax.axis_index("core") == 0
     copies = [
         pltpu.make_async_copy(source, target, sem.at[k])
-        for k, (source, target) in enumerate(((filt_ref, filt_out), (x_ref, x_out), (g_ref, g_out)))
+        for k, (source, target) in enumerate(
+            (
+                (filt_ref, filt_out),
+                (x_ref, x_out),
+                (g_ref.at[0:taps], g_out.at[0:taps]),
+                (g_ref.at[taps:rows], g_out.at[taps:rows]),
+            )
+        )
     ]
     for copy in copies:
         copy.start()
-    for copy in copies:
+    for copy in copies[:3]:
         copy.wait()
     for part, far_ref in enumerate(far_refs):
 
@@ -72,6 +79,7 @@
             return 0
 
         lax.fori_loop(0, width // LANES, tile, 0)
+    copies[3].wait()
 
 
 def edge_call(x, g, filters, taps, parts):
@@ -83,10 +91,10 @@
         in_specs=[pl.BlockSpec(memory_space=pltpu.HBM)] * 3,
         out_specs=[pl.BlockSpec(memory_space=pltpu.VMEM)] * (4 + parts),
         out_shape=same + [halo(chans)] + [halo(chans // parts)] * parts,
-        scratch_shapes=[pltpu.VMEM((taps + 8, LANES), F32), pltpu.SemaphoreType.DMA((3,))],
+        scratch_shapes=[pltpu.VMEM((taps + 8, LANES), F32), pltpu.SemaphoreType.DMA((4,))],
         compiler_params=pltpu.CompilerParams(vmem_limit_bytes=EDGE_LIMIT),
         name="edges",
-    )(x, g, filters)
+    )(*(pltpu.with_memory_space_constraint(a, pltpu.HBM) for a in (x, g, filters)))
     return made[:3], made[3], made[4:]
 
 
@@ -348,6 +356,15 @@
     )(x, g, near, far, filters, fwd, bwd)
 
 
+def spread_kernel(part_ref, all_ref):
+    rows = PER + 9
+    parts = [part_ref[k : k + rows, :] for k in range(0, part_ref.shape[0], rows)]
+    while len(parts) > 1:
+        parts = [a + b for a, b in zip(parts[::2], parts[1::2])]
+    for k in range(0, all_ref.shape[0], rows):
+        all_ref[k : k + rows, :] = parts[0]
+
+
 def unpack_kernel(part_ref, short_ref, long_ref):
     rows = PER + 9
     for tile in range(part_ref.shape[0] // rows):
@@ -370,14 +387,15 @@
 
 
 def summed(part, inner, outer):
+    rows, lanes = part.shape[1:]
     inner_size, outer_size = lax.axis_size(inner), lax.axis_size(outer)
-    shape = part.shape
-    part = part.reshape((inner_size, shape[0] // inner_size) + shape[1:])
-    part = jnp.sum(lax.all_to_all(part, inner, 0, 0, tiled=True), axis=0)
-    part = lax.optimization_barrier(jnp.broadcast_to(part[None], (outer_size,) + part.shape))
-    part = jnp.sum(lax.all_to_all(part, outer, 0, 0, tiled=True), axis=0)
-    part = lax.optimization_barrier(jnp.broadcast_to(part[None], (inner_size,) + part.shape))
-    return lax.all_to_all(part, inner, 0, 0, tiled=True).reshape(shape)
+    copies = lambda n: jax.ShapeDtypeStruct((n * rows, lanes), F32)
+    swap = lambda a, axes, n: lax.all_to_all(a.reshape(n, -1, rows, lanes), axes, 0, 0, tiled=True)
+    part = swap(part, inner, inner_size).reshape(-1, lanes)
+    part = on_vmem(spread_kernel, "sum_inner", copies(outer_size), part)
+    part = swap(part, outer, outer_size).reshape(-1, lanes)
+    part = on_vmem(spread_kernel, "sum_outer", copies(inner_size), part)
+    return swap(part, inner, inner_size)
 
 
 PARTS = 2

time: 90.8 us -> 88.1 us (0.970)
  local copies, waits for them, and re-layouts: 5.07 us -> 0.16 us
  Pallas kernels: 17.9 us -> 20.5 us
    unnamed x10 -> x4, local copies, waits for them, and re-layouts: 3.34 us -> 0.01 us
    broadcast_in_dim x2 -> x0, local copies, waits for them, and re-layouts: 1.58 us -> none  [the longest x1 0.85 us: summed(): jnp.broadcast_to(part[None], (outer_size,) + part.shape)]
    pallas_call x1 -> x3, Pallas kernels: 0.7 us -> 2.14 us  [on_vmem(): pl.pallas_call(kernel, in_specs=[pl.BlockSpec(memory_space=pltpu.VMEM)] *...]
    pallas_call x1, Pallas kernels: 1.08 us -> 2.29 us  [edge_call(): pl.pallas_call(edge_kernel, in_specs=[pl.BlockSpec(memory_space=pltpu.HBM...]
  transfers between devices with their start and end apart: 6 -> 6, of which waited for: 4 -> 4; matrix products, arithmetic and copies ran while one was open for 1% -> 0% of each run, Pallas kernels for 11% -> 12%
where the time goes in v3:
time: 88.1 us; the launch traced here: 87 us
  starting transfers between devices  40.4 us (46%)
  Pallas kernels  20.5 us (23%)
  waiting for transfers between devices  17 us (19%)
  blocking collectives  7.96 us (9%)
    all_to_all x2, starting transfers between devices, summed(): lax.all_to_all(a.reshape(n, -1, rows, lanes), axes, 0, 0, tiled=True)  21.8 us
    all_to_all x2, waiting for transfers between devices, summed(): lax.all_to_all(a.reshape(n, -1, rows, lanes), axes, 0, 0, tiled=True)  13.9 us
    pallas_call x2, Pallas kernels, main_call(): pl.pallas_call(functools.partial(main_kernel, (width, part, CHUNK, PIECE)...  12.4 us
    ppermute x1, starting transfers between devices, local(): near = lax.ppermute(near, SEQ, within)  8.79 us
    all_to_all x1, blocking collectives, summed(): lax.all_to_all(a.reshape(n, -1, rows, lanes), axes, 0, 0, tiled=True)  7.96 us
    ppermute x2, starting transfers between devices, local(): far = [lax.ppermute(rows_of, SEQ, between) for rows_of in far]  6.46 us
    pallas_call x1, Pallas kernels, table_call(): pl.pallas_call(table_kernel, in_specs=[pl.BlockSpec(memory_space=pltpu.VM...  3.74 us
    ppermute x1, starting transfers between devices, local(): head = lax.ppermute(head[:2], SEQ, back)  3.33 us
  transfers between devices with their start and end apart: 6, of which 4 were waited for; matrix products, arithmetic and copies ran while one was open for 0% of the time, Pallas kernels for 12%

profile of v3, /device:TPU:1, one launch (start us, length us, event | category | flops | bytes accessed | tf_op | source)
XLA Modules:
  0.0 87.0 jit_solution(3996817426577930860)
XLA Ops:
  0.6 0.0 copy-start
  0.6 2.3 %edges.1 = (bf16[256,2048]{1,0:T(8,128)(2,1)S(1)}, bf16[256,2048]{1,0:T(8,128)(2,1)S(1)}, f32[3,3,2048]{2,1,0:T(4,128)S(1)}, bf16[144,2048]{1,0:T(8,128)(2,1)S(1...) custom-call(bf16[256,2048]{1,0:T(8,128)(2,1)} %bitcast.16, bf16[256,2048]{1,0:T(8,128)(2,1)} %bitcast.17, ...), custom_call_target="tpu_custom_call" | custom-call | tf_op jit(solution)/shard_map/edges/pallas_call | solution.py:89
  2.9 8.8 %collective-permute-start = (bf16[144,2048]{1,0:T(8,128)(2,1)S(1)}, bf16[144,2048]{1,0:T(8,128)(2,1)S(1)}, u32[]{:S(2)}, u32[]{:S(2)}) collective-permute-start(bf16[144,2048]{1,0:T(8,128)(2,1)S(1)} %get-tuple-element.23), channel_id=1, source_target_pairs={{0,8},{8,0},{16,24},{24,16},{32,40},{40,32},{48,56},{56,48},{64,72... | collective-permute-start | bytes 1769480 | tf_op jit(solution)/shard_map/ppermute | solution.py:417
  11.7 1.9 %collective-permute-start.2 = (bf16[144,1024]{1,0:T(8,128)(2,1)S(1)}, bf16[144,1024]{1,0:T(8,128)(2,1)S(1)}, u32[]{:S(2)}, u32[]{:S(2)}) collective-permute-start(bf16[144,1024]{1,0:T(8,128)(2,1)S(1)} %get-tuple-element.29), channel_id=1, source_target_pairs={{8,16},{24,32},{40,48},{56,64},{72,80},{88,96},{104,112},{120,128}... | collective-permute-start | bytes 884744 | tf_op jit(solution)/shard_map/ppermute | solution.py:418
  13.7 4.5 %collective-permute-start.1 = (bf16[144,1024]{1,0:T(8,128)(2,1)S(1)}, bf16[144,1024]{1,0:T(8,128)(2,1)S(1)}, u32[]{:S(2)}, u32[]{:S(2)}) collective-permute-start(bf16[144,1024]{1,0:T(8,128)(2,1)S(1)} %get-tuple-element.24), channel_id=1, source_target_pairs={{8,16},{24,32},{40,48},{56,64},{72,80},{88,96},{104,112},{120,128}... | collective-permute-start | bytes 884744 | tf_op jit(solution)/shard_map/ppermute | solution.py:418
  18.2 0.0 copy-done
  18.2 3.7 %tables.1 = (bf16[16384,256]{1,0:T(8,128)(2,1)S(1)}, bf16[16384,256]{1,0:T(8,128)(2,1)S(1)}) custom-call(f32[128,128]{1,0:T(8,128)S(1)} %copy-done), custom_call_target="tpu_custom_call" | custom-call | flops 83886080 | bytes 16777216 | tf_op jit(solution)/shard_map/tables/pallas_call | solution.py:134
  22.0 2.9 %collective-permute-done.2.far_ref = bf16[144,1024]{1,0:T(8,128)(2,1)S(1)} collective-permute-done((bf16[144,1024]{1,0:T(8,128)(2,1)S(1)}, bf16[144,1024]{1,0:T(8,128)(2,1)S(1)}, u32[]{:S(2)}, u32[]{:S(2)}) %collective-permute-start.2) | collective-permute-done | bytes 294944 | tf_op jit(solution)/shard_map/ppermute | solution.py:418
  24.9 0.0 collective-permute-done.near_ref
  24.9 6.2 %operator.3 = (bf16[256,1024]{1,0:T(8,128)(2,1)S(1)}, f32[8,1024]{1,0:T(8,128)S(1)}, f32[8,1024]{1,0:T(8,128)S(1)}, f32[8,17,128]{2,1,0:T(8,128)S(1)}) custom-call(bf16[256,2048]{1,0:T(8,128)(2,1)S(1)} %get-tuple-element.21.x_ref, bf16[256,2048]{1,0:T(8,128)(2,1)S(1)} %get-tuple-element.22.g_ref, bf16[144,2048]{1,0:T(8,128)(2,1)S(1)} %collective-permute-done.near_ref, ...), custom_call_target="tpu_custom_call" | custom-call | flops 25999998976 | bytes 25165824 | tf_op jit(solution)/shard_map/operator/pallas_call | solution.py:341
  31.1 0.2 collective-permute-done.1.far_ref
  31.3 6.2 %operator.2 = (bf16[256,1024]{1,0:T(8,128)(2,1)S(1)}, f32[8,1024]{1,0:T(8,128)S(1)}, f32[8,1024]{1,0:T(8,128)S(1)}, f32[8,17,128]{2,1,0:T(8,128)S(1)}) custom-call(bf16[256,2048]{1,0:T(8,128)(2,1)S(1)} %get-tuple-element.21.x_ref, bf16[256,2048]{1,0:T(8,128)(2,1)S(1)} %get-tuple-element.22.g_ref, bf16[144,2048]{1,0:T(8,128)(2,1)S(1)} %collective-permute-done.near_ref, ...), custom_call_target="tpu_custom_call" | custom-call | flops 25999998976 | bytes 25165824 | tf_op jit(solution)/shard_map/operator/pallas_call | solution.py:341
  37.5 0.1 copy.7
  37.6 8.0 %all_to_all.15 = f32[16,1,17,128]{3,1,2,0:T(1,128)S(1)} all-to-all(f32[16,1,17,128]{3,1,2,0:T(1,128)S(1)} %copy.7), channel_id=1, replica_groups=mesh['y'=8,'z_hi'=4,'core'=2,'x'=4,'z_lo'=2] {'core','x','z_lo'}, dimensions={0} | all-to-all | bytes 278528 | tf_op jit(solution)/shard_map/all_to_all | solution.py:393
  45.6 0.7 sum_inner.1
  46.4 15.2 %all-to-all-start.1 = ((f32[32,1,17,128]{3,1,2,0:T(1,128)}), f32[32,1,17,128]{3,1,2,0:T(1,128)S(1)}, u32[]{:S(2)}, u32[]{:S(2)}) async-start(f32[32,1,17,128]{3,1,2,0:T(1,128)} %bitcast.6), calls=%async_computation.1 | async-start | bytes 557056 | tf_op jit(solution)/shard_map/all_to_all | solution.py:393
  61.5 3.3 %collective-permute-start.3 = (f32[2,2048]{1,0:T(2,128)S(1)}, f32[2,2048]{1,0:T(2,128)S(1)}, u32[]{:S(2)}, u32[]{:S(2)}) collective-permute-start(f32[2,2048]{1,0:T(2,128)S(1)} %pad_maximum_fusion), channel_id=1, source_target_pairs={{8,0},{16,8},{24,16},{32,24},{40,32},{48,40},{56,48},{64,56},{72,6... | collective-permute-start | bytes 49160 | tf_op jit(solution)/shard_map/ppermute | solution.py:427
  64.9 0.1 maximum_bitcast_fusion
  65.0 8.2 %all-to-all-done.1 = f32[32,1,17,128]{3,1,2,0:T(1,128)S(1)} async-done(((f32[32,1,17,128]{3,1,2,0:T(1,128)}), f32[32,1,17,128]{3,1,2,0:T(1,128)S(1)}, u32[]{:S(2)}, u32[]{:S(2)}) %all-to-all-start.1) | async-done | bytes 278560 | tf_op jit(solution)/shard_map/all_to_all | solution.py:393
  73.2 0.7 sum_outer.1
  73.9 6.7 %all-to-all-start.2 = ((f32[16,1,17,128]{3,1,2,0:T(1,128)}), f32[16,1,17,128]{3,1,2,0:T(1,128)S(1)}, u32[]{:S(2)}, u32[]{:S(2)}) async-start(f32[16,1,17,128]{3,1,2,0:T(1,128)} %bitcast.8), calls=%async_computation.2 | async-start | bytes 278528 | tf_op jit(solution)/shard_map/all_to_all | solution.py:393
  80.6 0.0 collective-permute-done.3
  80.6 0.0 copy-start.1
  80.6 5.7 %all-to-all-done.2 = f32[16,1,17,128]{3,1,2,0:T(1,128)S(1)} async-done(((f32[16,1,17,128]{3,1,2,0:T(1,128)}), f32[16,1,17,128]{3,1,2,0:T(1,128)S(1)}, u32[]{:S(2)}, u32[]{:S(2)}) %all-to-all-start.2) | async-done | bytes 139296 | tf_op jit(solution)/shard_map/all_to_all | solution.py:393
  86.3 0.7 unpack.1
  87.0 0.0 copy-done.1
  (3 shorter events, 0.1 us)
Async XLA Ops:
  0.6 17.6 %copy-start = (f32[128,128]{1,0:T(8,128)S(1)}, f32[128,128]{1,0:T(8,128)}, u32[]{:S(2)}) copy-start(f32[128,128]{1,0:T(8,128)} %filter_ref.1) | copy-start | bytes 196612
  2.9 22.0 %collective-permute-start = (bf16[144,2048]{1,0:T(8,128)(2,1)S(1)}, bf16[144,2048]{1,0:T(8,128)(2,1)S(1)}, u32[]{:S(2)}, u32[]{:S(2)}) collective-permute-start(bf16[144,2048]{1,0:T(8,128)(2,1)S(1)} %get-tuple-element.23), channel_id=1, source_target_pairs={{0,8},{8,0},{16,24},{24,16},{32,40},{40,32},{48,56},{56,48},{64,72... | collective-permute-start | bytes 1769480 | tf_op jit(solution)/shard_map/ppermute | solution.py:417
  11.7 13.2 %collective-permute-start.2 = (bf16[144,1024]{1,0:T(8,128)(2,1)S(1)}, bf16[144,1024]{1,0:T(8,128)(2,1)S(1)}, u32[]{:S(2)}, u32[]{:S(2)}) collective-permute-start(bf16[144,1024]{1,0:T(8,128)(2,1)S(1)} %get-tuple-element.29), channel_id=1, source_target_pairs={{8,16},{24,32},{40,48},{56,64},{72,80},{88,96},{104,112},{120,128}... | collective-permute-start | bytes 884744 | tf_op jit(solution)/shard_map/ppermute | solution.py:418
  13.7 17.6 %collective-permute-start.1 = (bf16[144,1024]{1,0:T(8,128)(2,1)S(1)}, bf16[144,1024]{1,0:T(8,128)(2,1)S(1)}, u32[]{:S(2)}, u32[]{:S(2)}) collective-permute-start(bf16[144,1024]{1,0:T(8,128)(2,1)S(1)} %get-tuple-element.24), channel_id=1, source_target_pairs={{8,16},{24,32},{40,48},{56,64},{72,80},{88,96},{104,112},{120,128}... | collective-permute-start | bytes 884744 | tf_op jit(solution)/shard_map/ppermute | solution.py:418
  46.4 26.8 %all-to-all-start.1 = ((f32[32,1,17,128]{3,1,2,0:T(1,128)}), f32[32,1,17,128]{3,1,2,0:T(1,128)S(1)}, u32[]{:S(2)}, u32[]{:S(2)}) async-start(f32[32,1,17,128]{3,1,2,0:T(1,128)} %bitcast.6), calls=%async_computation.1 | async-start | bytes 557056 | tf_op jit(solution)/shard_map/all_to_all | solution.py:393
  61.5 19.0 %collective-permute-start.3 = (f32[2,2048]{1,0:T(2,128)S(1)}, f32[2,2048]{1,0:T(2,128)S(1)}, u32[]{:S(2)}, u32[]{:S(2)}) collective-permute-start(f32[2,2048]{1,0:T(2,128)S(1)} %pad_maximum_fusion), channel_id=1, source_target_pairs={{8,0},{16,8},{24,16},{32,24},{40,32},{48,40},{56,48},{64,56},{72,6... | collective-permute-start | bytes 49160 | tf_op jit(solution)/shard_map/ppermute | solution.py:427
  73.9 12.5 %all-to-all-start.2 = ((f32[16,1,17,128]{3,1,2,0:T(1,128)}), f32[16,1,17,128]{3,1,2,0:T(1,128)S(1)}, u32[]{:S(2)}, u32[]{:S(2)}) async-start(f32[16,1,17,128]{3,1,2,0:T(1,128)} %bitcast.8), calls=%async_computation.2 | async-start | bytes 278528 | tf_op jit(solution)/shard_map/all_to_all | solution.py:393
  80.6 6.4 %copy-start.1 = (bf16[1,256,2048]{2,1,0:T(8,128)(2,1)}, bf16[1,256,2048]{2,1,0:T(8,128)(2,1)S(1)}, u32[]{:S(2)}) copy-start(bf16[1,256,2048]{2,1,0:T(8,128)(2,1)S(1)} %bitcast_dynamic-update-slice_fusion) | copy-start | bytes 3145732

commit v4 on v3

--- a/solution.py
+++ b/solution.py
@@ -154,18 +154,15 @@
     filt_ref,
     fwd_ref,
     bwd_ref,
-    out_ref,
-    rim_ref,
-    head_ref,
+    query_ref,
+    key_ref,
+    value_ref,
     packed_ref,
     ext,
     key_s,
     value_s,
     prod_s,
     grad_s,
-    lag0,
-    lag1,
-    lag2,
     fold,
 ):
     rows, width = x_ref.shape[0], cfg[0]
@@ -179,9 +176,7 @@
     row = lax.broadcasted_iota(jnp.int32, (taps, taps), 0)
     col = lax.broadcasted_iota(jnp.int32, (taps, taps), 1)
     below = col <= row
-    head_ref[2:, :] = jnp.zeros((6, head_ref.shape[1]), F32)
-
-    chans = out_ref.shape[1]
+    chans = query_ref.shape[1]
     skip = cfg[1] * chans
 
     def lanes_of(tile):
@@ -222,7 +217,6 @@
 
     def work(tile, sub):
         at, of = lanes_of(tile)
-        taken = filters(of)
         window = jnp.concatenate([prod_s[sub, 0 : 2 * taps, :], prod_s[sub, taps:, :]], axis=1)
         after = jnp.concatenate([grad_s[sub, 0 : 2 * taps, :], grad_s[sub, taps:, :]], axis=1)
         both = jnp.concatenate([grad_s[sub, 0:taps, :], grad_s[sub, taps : 2 * taps, :]], axis=1)
@@ -255,8 +249,8 @@
                     for i in range(3):
                         term = grads[i] * shifted
                         sums[3 * i + lag] += sum(term[k : k + 8] for k in range(0, CHUNK, 8))
-                for lag, keep in enumerate((lag0, lag1, lag2)):
-                    keep[sub, here, :] = sum(taken[i][lag] * grads[i] for i in range(3))
+                for keep, grad in zip((query_ref, key_ref, value_ref), grads):
+                    keep[here, at] = grad
                 yield
             masked = jnp.concatenate(
                 [
@@ -289,22 +283,7 @@
             total = total + pltpu.roll(fold[sub, pl.ds(r, PER, stride=8), :], taps - r, 1)
         turn = (taps - lax.broadcasted_iota(jnp.int32, (PER, taps), 1)) % taps
         packed_ref[tile, 0:PER, :] = jnp.take_along_axis(total, turn, axis=1) * scale
-        lag1[sub, rows:, :] = jnp.zeros((8, LANES), F32)
-        lag2[sub, rows:, :] = jnp.zeros((8, LANES), F32)
         yield
-        for start in range(0, rows, PIECE):
-            here = slice(start, start + PIECE)
-            total = (
-                lag0[sub, here, :]
-                + lag1[sub, start + 1 : start + 1 + PIECE, :]
-                + lag2[sub, start + 2 : start + 2 + PIECE, :]
-            )
-            out_ref[here, at] = total.astype(BF16)
-            if start == rows - PIECE:
-                rim_ref[:, at] = total[PIECE - 8 :, :]
-            yield
-        head_ref[0:1, at] = lag2[sub, 0:1, :]
-        head_ref[1:2, at] = lag1[sub, 0:1, :] + lag2[sub, 1:2, :]
 
     tiles = chans // LANES
 
@@ -343,17 +322,66 @@
         in_specs=[pl.BlockSpec(memory_space=pltpu.VMEM)] * 7,
         out_specs=[pl.BlockSpec(memory_space=pltpu.VMEM)] * 4,
         out_shape=[
-            jax.ShapeDtypeStruct((rows, chans), BF16), f32(8, chans), f32(8, chans),
+            f32(rows, chans), f32(rows, chans), f32(rows, chans),
             f32(chans // LANES, PER + 9, taps),
         ],
         scratch_shapes=[
             wide(lead + rows + 8), wide(rows), wide(rows), wide(rows + taps, BF16),
-            wide(rows + taps, BF16), wide(rows), wide(rows + 8), wide(rows + 8), wide(8 * PER),
+            wide(rows + taps, BF16), wide(8 * PER),
         ],
         compiler_params=pltpu.CompilerParams(vmem_limit_bytes=VMEM_LIMIT),
         cost_estimate=pl.CostEstimate(flops=26 * 10**9, bytes_accessed=24 * 2**20, transcendentals=0),
         name="operator",
     )(x, g, near, far, filters, fwd, bwd)
+
+
+def mix_kernel(*refs):
+    grads, filt_ref = refs[:-8], refs[-8]
+    out_ref, rim_ref, head_ref, lag0, lag1, lag2 = refs[-6:]
+    rows, width = grads[0].shape
+    pieces = [slice(start, start + PIECE) for start in range(0, rows, PIECE)]
+    head_ref[2:, :] = jnp.zeros((6, head_ref.shape[1]), F32)
+    lag1[rows:, :] = jnp.zeros((8, LANES), F32)
+    lag2[rows:, :] = jnp.zeros((8, LANES), F32)
+    for part in range(len(grads) // 3):
+
+        def tile(i, _):
+            there = pl.ds(pl.multiple_of(i * LANES, LANES), LANES)
+            at = pl.ds(pl.multiple_of(part * width + i * LANES, LANES), LANES)
+            for here in pieces:
+                branches = [ref[here, there] for ref in grads[3 * part : 3 * part + 3]]
+                for lag, keep in enumerate((lag0, lag1, lag2)):
+                    keep[here, :] = sum(filt_ref[k, lag : lag + 1, at] * branches[k] for k in range(3))
+            for here in pieces:
+                start = here.start
+                total = (
+                    lag0[here, :]
+                    + lag1[start + 1 : start + 1 + PIECE, :]
+                    + lag2[start + 2 : start + 2 + PIECE, :]
+                )
+                out_ref[here, at] = total.astype(BF16)
+                if here is pieces[-1]:
+                    rim_ref[:, at] = total[PIECE - 8 :, :]
+            head_ref[0:1, at] = lag2[0:1, :]
+            head_ref[1:2, at] = lag1[0:1, :] + lag2[1:2, :]
+            return 0
+
+        lax.fori_loop(0, width // LANES, tile, 0)
+
+
+def mix_call(grads, filters, after):
+    rows, chans = grads[0].shape[0], filters.shape[2]
+    f32 = lambda *shape: jax.ShapeDtypeStruct(shape, F32)
+    return pl.pallas_call(
+        mix_kernel,
+        in_specs=[pl.BlockSpec(memory_space=pltpu.VMEM)] * (len(grads) + 1)
+        + [pl.BlockSpec(memory_space=pl.ANY)],
+        out_specs=[pl.BlockSpec(memory_space=pltpu.VMEM)] * 3,
+        out_shape=[jax.ShapeDtypeStruct((rows, chans), BF16), f32(8, chans), f32(8, chans)],
+        scratch_shapes=[pltpu.VMEM((rows + 8, LANES), F32)] * 3,
+        compiler_params=pltpu.CompilerParams(vmem_limit_bytes=TABLE_LIMIT),
+        name="mix",
+    )(*(pltpu.with_memory_space_constraint(a, pltpu.VMEM) for a in grads), filters, after)
 
 
 def spread_kernel(part_ref, all_ref):
@@ -393,9 +421,10 @@
     swap = lambda a, axes, n: lax.all_to_all(a.reshape(n, -1, rows, lanes), axes, 0, 0, tiled=True)
     part = swap(part, inner, inner_size).reshape(-1, lanes)
     part = on_vmem(spread_kernel, "sum_inner", copies(outer_size), part)
+    early = part
     part = swap(part, outer, outer_size).reshape(-1, lanes)
     part = on_vmem(spread_kernel, "sum_outer", copies(inner_size), part)
-    return swap(part, inner, inner_size)
+    return swap(part, inner, inner_size), early
 
 
 PARTS = 2
@@ -421,13 +450,12 @@
         main_call(x, g, near, far[k], filters, fwd, bwd, WIDTH, scale, k)
         for k in range(PARTS)
     ]
-    out, rim, head, packed = (
-        jnp.concatenate([d[i] for d in done], axis=(1, 1, 1, 0)[i]) for i in range(4)
-    )
+    packed = jnp.concatenate([d[3] for d in done], axis=0)
+    packed, early = summed(packed, ("core", "x", "z_lo"), ("y", "z_hi"))
+    out, rim, head = mix_call([grad for d in done for grad in d[:3]], filters, early)
     head = lax.ppermute(head[:2], SEQ, back)
     rim = (rim[6:] + head).astype(BF16)
     out = lax.dynamic_update_slice(out, rim, (rows - 2, 0))
-    packed = summed(packed, ("core", "x", "z_lo"), ("y", "z_hi"))
     short, long = on_vmem(
         unpack_kernel,
         "unpack",

time: 88.1 us -> 89.5 us (1.016)
  waiting for transfers between devices: 17 us -> 8.92 us
  local copies, waits for them, and re-layouts: 0.16 us -> 8.23 us
  other arithmetic: 0.14 us -> 1.47 us
    all_to_all x2, waiting for transfers between devices: 13.9 us -> 5.81 us  [summed(): lax.all_to_all(a.reshape(n, -1, rows, lanes), axes, 0, 0, tiled=True)]
    unnamed x4 -> x16, local copies, waits for them, and re-layouts: 0.01 us -> 8.08 us
    pallas_call x0 -> x1, Pallas kernels: none -> 2.51 us  [mix_call(): pl.pallas_call(mix_kernel, in_specs=[pl.BlockSpec(memory_space=pltpu.VMEM...]
    pallas_call x2, Pallas kernels: 12.4 us -> 10.7 us  [main_call(): pl.pallas_call(functools.partial(main_kernel, (width, part, CHUNK, PIECE)...]
    dynamic_update_slice x1, other arithmetic: 0.02 us -> 1.45 us  [local(): out = lax.dynamic_update_slice(out, rim, (rows - 2, 0))]
  transfers between devices with their start and end apart: 6 -> 6, of which waited for: 4 -> 4; matrix products, arithmetic and copies ran while one was open for 0% -> 2% of each run, Pallas kernels for 12% -> 14%
where the time goes in v4:
time: 89.5 us; the launch traced here: 88.2 us
  starting transfers between devices  40.1 us (45%)
  Pallas kernels  21.3 us (24%)
  waiting for transfers between devices  8.92 us (10%)
  local copies, waits for them, and re-layouts  8.23 us (9%)
  blocking collectives  7.39 us (8%)
  other arithmetic  1.47 us (2%)
    all_to_all x2, starting transfers between devices, summed(): lax.all_to_all(a.reshape(n, -1, rows, lanes), axes, 0, 0, tiled=True)  21.6 us
    pallas_call x2, Pallas kernels, main_call(): pl.pallas_call(functools.partial(main_kernel, (width, part, CHUNK, PIECE)...  10.7 us
    ppermute x1, starting transfers between devices, local(): near = lax.ppermute(near, SEQ, within)  8.79 us
    unnamed x16, local copies, waits for them, and re-layouts  8.08 us
    all_to_all x1, blocking collectives, summed(): lax.all_to_all(a.reshape(n, -1, rows, lanes), axes, 0, 0, tiled=True)  7.39 us
    ppermute x2, starting transfers between devices, local(): far = [lax.ppermute(rows_of, SEQ, between) for rows_of in far]  6.46 us
    all_to_all x2, waiting for transfers between devices, summed(): lax.all_to_all(a.reshape(n, -1, rows, lanes), axes, 0, 0, tiled=True)  5.81 us
    pallas_call x1, Pallas kernels, table_call(): pl.pallas_call(table_kernel, in_specs=[pl.BlockSpec(memory_space=pltpu.VM...  3.73 us
  transfers between devices with their start and end apart: 6, of which 4 were waited for; matrix products, arithmetic and copies ran while one was open for 2% of the time, Pallas kernels for 14%

profile of v4, /device:TPU:1, one launch (start us, length us, event | category | flops | bytes accessed | tf_op | source)
XLA Modules:
  0.0 88.2 jit_solution(15887566238760811577)
XLA Ops:
  0.6 2.3 %edges.1 = (bf16[256,2048]{1,0:T(8,128)(2,1)S(1)}, bf16[256,2048]{1,0:T(8,128)(2,1)S(1)}, f32[3,3,2048]{2,1,0:T(4,128)S(1)}, bf16[144,2048]{1,0:T(8,128)(2,1)S(1...) custom-call(bf16[256,2048]{1,0:T(8,128)(2,1)} %bitcast.17, bf16[256,2048]{1,0:T(8,128)(2,1)} %bitcast.18, ...), custom_call_target="tpu_custom_call" | custom-call | tf_op jit(solution)/shard_map/edges/pallas_call | solution.py:89
  2.9 8.8 %collective-permute-start = (bf16[144,2048]{1,0:T(8,128)(2,1)S(1)}, bf16[144,2048]{1,0:T(8,128)(2,1)S(1)}, u32[]{:S(2)}, u32[]{:S(2)}) collective-permute-start(bf16[144,2048]{1,0:T(8,128)(2,1)S(1)} %get-tuple-element.26), channel_id=1, source_target_pairs={{0,8},{8,0},{16,24},{24,16},{32,40},{40,32},{48,56},{56,48},{64,72... | collective-permute-start | bytes 1769480 | tf_op jit(solution)/shard_map/ppermute | solution.py:446
  11.7 1.9 %collective-permute-start.2 = (bf16[144,1024]{1,0:T(8,128)(2,1)S(1)}, bf16[144,1024]{1,0:T(8,128)(2,1)S(1)}, u32[]{:S(2)}, u32[]{:S(2)}) collective-permute-start(bf16[144,1024]{1,0:T(8,128)(2,1)S(1)} %get-tuple-element.34), channel_id=1, source_target_pairs={{8,16},{24,32},{40,48},{56,64},{72,80},{88,96},{104,112},{120,128}... | collective-permute-start | bytes 884744 | tf_op jit(solution)/shard_map/ppermute | solution.py:447
  13.6 4.5 %collective-permute-start.1 = (bf16[144,1024]{1,0:T(8,128)(2,1)S(1)}, bf16[144,1024]{1,0:T(8,128)(2,1)S(1)}, u32[]{:S(2)}, u32[]{:S(2)}) collective-permute-start(bf16[144,1024]{1,0:T(8,128)(2,1)S(1)} %get-tuple-element.27), channel_id=1, source_target_pairs={{8,16},{24,32},{40,48},{56,64},{72,80},{88,96},{104,112},{120,128}... | collective-permute-start | bytes 884744 | tf_op jit(solution)/shard_map/ppermute | solution.py:447
  18.2 0.0 copy-start.7
  18.2 0.8 copy-done.7
  19.0 3.7 %tables.1 = (bf16[16384,256]{1,0:T(8,128)(2,1)S(1)}, bf16[16384,256]{1,0:T(8,128)(2,1)S(1)}) custom-call(f32[128,128]{1,0:T(8,128)S(1)} %copy-done.7), custom_call_target="tpu_custom_call" | custom-call | flops 83886080 | bytes 16777216 | tf_op jit(solution)/shard_map/tables/pallas_call | solution.py:134
  22.8 2.1 %collective-permute-done.2.far_ref = bf16[144,1024]{1,0:T(8,128)(2,1)S(1)} collective-permute-done((bf16[144,1024]{1,0:T(8,128)(2,1)S(1)}, bf16[144,1024]{1,0:T(8,128)(2,1)S(1)}, u32[]{:S(2)}, u32[]{:S(2)}) %collective-permute-start.2) | collective-permute-done | bytes 294944 | tf_op jit(solution)/shard_map/ppermute | solution.py:447
  24.9 0.0 collective-permute-done.near_ref
  24.9 5.4 %operator.3 = (f32[256,1024]{1,0:T(8,128)S(1)}, f32[256,1024]{1,0:T(8,128)S(1)}, f32[256,1024]{1,0:T(8,128)S(1)}, f32[8,17,128]{2,1,0:T(8,128)S(1)}) custom-call(bf16[256,2048]{1,0:T(8,128)(2,1)S(1)} %get-tuple-element.24.x_ref, bf16[256,2048]{1,0:T(8,128)(2,1)S(1)} %get-tuple-element.25.g_ref, bf16[144,2048]{1,0:T(8,128)(2,1)S(1)} %collective-permute-done.near_ref, ...), custom_call_target="tpu_custom_call" | custom-call | flops 25999998976 | bytes 25165824 | tf_op jit(solution)/shard_map/operator/pallas_call | solution.py:320
  30.2 1.0 %collective-permute-done.1.far_ref = bf16[144,1024]{1,0:T(8,128)(2,1)S(1)} collective-permute-done((bf16[144,1024]{1,0:T(8,128)(2,1)S(1)}, bf16[144,1024]{1,0:T(8,128)(2,1)S(1)}, u32[]{:S(2)}, u32[]{:S(2)}) %collective-permute-start.1) | collective-permute-done | bytes 294944 | tf_op jit(solution)/shard_map/ppermute | solution.py:447
  31.2 5.4 %operator.2 = (f32[256,1024]{1,0:T(8,128)S(1)}, f32[256,1024]{1,0:T(8,128)S(1)}, f32[256,1024]{1,0:T(8,128)S(1)}, f32[8,17,128]{2,1,0:T(8,128)S(1)}) custom-call(bf16[256,2048]{1,0:T(8,128)(2,1)S(1)} %get-tuple-element.24.x_ref, bf16[256,2048]{1,0:T(8,128)(2,1)S(1)} %get-tuple-element.25.g_ref, bf16[144,2048]{1,0:T(8,128)(2,1)S(1)} %collective-permute-done.near_ref, ...), custom_call_target="tpu_custom_call" | custom-call | flops 25999998976 | bytes 25165824 | tf_op jit(solution)/shard_map/operator/pallas_call | solution.py:320
  36.6 0.0 copy-start
  36.6 1.0 %copy-done = f32[256,1024]{1,0:T(8,128)} copy-done((f32[256,1024]{1,0:T(8,128)}, f32[256,1024]{1,0:T(8,128)S(1)}, u32[]{:S(2)}) %copy-start) | copy-done | bytes 1048600
  37.6 0.0 copy-start.2
  37.6 1.0 %copy-done.2 = f32[256,1024]{1,0:T(8,128)} copy-done((f32[256,1024]{1,0:T(8,128)}, f32[256,1024]{1,0:T(8,128)S(1)}, u32[]{:S(2)}) %copy-start.2) | copy-done | bytes 1048600
  38.5 0.0 copy-start.4
  38.6 1.0 %copy-done.4 = f32[256,1024]{1,0:T(8,128)} copy-done((f32[256,1024]{1,0:T(8,128)}, f32[256,1024]{1,0:T(8,128)S(1)}, u32[]{:S(2)}) %copy-start.4) | copy-done | bytes 1048600
  39.5 0.1 copy.7
  39.7 7.4 %all_to_all.15 = f32[16,1,17,128]{3,1,2,0:T(1,128)S(1)} all-to-all(f32[16,1,17,128]{3,1,2,0:T(1,128)S(1)} %copy.7), channel_id=1, replica_groups=mesh['y'=8,'z_hi'=4,'core'=2,'x'=4,'z_lo'=2] {'core','x','z_lo'}, dimensions={0} | all-to-all | bytes 278528 | tf_op jit(solution)/shard_map/all_to_all | solution.py:421
  47.1 0.8 sum_inner.1.refs_7_
  47.8 14.9 %all-to-all-start.1 = ((f32[32,1,17,128]{3,1,2,0:T(1,128)}), f32[32,1,17,128]{3,1,2,0:T(1,128)S(1)}, u32[]{:S(2)}, u32[]{:S(2)}) async-start(f32[32,1,17,128]{3,1,2,0:T(1,128)} %bitcast.6), calls=%async_computation.1 | async-start | bytes 557056 | tf_op jit(solution)/shard_map/all_to_all | solution.py:421
  62.7 0.0 copy-start.1
  62.7 1.2 %copy-done.1 = f32[256,1024]{1,0:T(8,128)S(1)} copy-done((f32[256,1024]{1,0:T(8,128)S(1)}, f32[256,1024]{1,0:T(8,128)}, u32[]{:S(2)}) %copy-start.1) | copy-done | bytes 1048600
  64.0 0.0 copy-start.3
  64.0 1.2 %copy-done.3 = f32[256,1024]{1,0:T(8,128)S(1)} copy-done((f32[256,1024]{1,0:T(8,128)S(1)}, f32[256,1024]{1,0:T(8,128)}, u32[]{:S(2)}) %copy-start.3) | copy-done | bytes 1048600
  65.2 0.0 copy-start.5
  65.2 1.2 %copy-done.5 = f32[256,1024]{1,0:T(8,128)S(1)} copy-done((f32[256,1024]{1,0:T(8,128)S(1)}, f32[256,1024]{1,0:T(8,128)}, u32[]{:S(2)}) %copy-start.5) | copy-done | bytes 1048600
  66.4 2.5 %mix.1 = (bf16[256,2048]{1,0:T(8,128)(2,1)}, f32[8,2048]{1,0:T(8,128)S(1)}, f32[8,2048]{1,0:T(8,128)S(1)}) custom-call(f32[256,1024]{1,0:T(8,128)S(1)} %copy-done.1, f32[256,1024]{1,0:T(8,128)S(1)} %copy-done.3, f32[256,1024]{1,0:T(8,128)S(1)} %copy-done.5, f32[256,1024]{1,0:T(8,128)S(1)} %get-tuple-element.35.refs_3_, ...), custom_call_target="tpu_custom_call" | custom-call | tf_op jit(solution)/shard_map/mix/pallas_call | solution.py:375
  68.9 0.0 copy-start.6
  68.9 0.6 copy-done.6
  69.5 3.3 %collective-permute-start.3 = (f32[2,2048]{1,0:T(2,128)S(1)}, f32[2,2048]{1,0:T(2,128)S(1)}, u32[]{:S(2)}, u32[]{:S(2)}) collective-permute-start(f32[2,2048]{1,0:T(2,128)S(1)} %slice.7), channel_id=1, source_target_pairs={{8,0},{16,8},{24,16},{32,24},{40,32},{48,40},{56,48},{64,56},{72,6... | collective-permute-start | bytes 49160 | tf_op jit(solution)/shard_map/ppermute | solution.py:456
  72.9 1.5 %all-to-all-done.1 = f32[32,1,17,128]{3,1,2,0:T(1,128)S(1)} async-done(((f32[32,1,17,128]{3,1,2,0:T(1,128)}), f32[32,1,17,128]{3,1,2,0:T(1,128)S(1)}, u32[]{:S(2)}, u32[]{:S(2)}) %all-to-all-start.1) | async-done | bytes 278560 | tf_op jit(solution)/shard_map/all_to_all | solution.py:421
  74.4 0.7 sum_outer.1
  75.1 6.7 %all-to-all-start.2 = ((f32[16,1,17,128]{3,1,2,0:T(1,128)}), f32[16,1,17,128]{3,1,2,0:T(1,128)S(1)}, u32[]{:S(2)}, u32[]{:S(2)}) async-start(f32[16,1,17,128]{3,1,2,0:T(1,128)} %bitcast.8), calls=%async_computation.2 | async-start | bytes 278528 | tf_op jit(solution)/shard_map/all_to_all | solution.py:421
  81.8 0.0 collective-permute-done.3
  81.8 1.5 %fusion.1 = bf16[1,256,2048]{2,1,0:T(8,128)(2,1)} fusion(bf16[1,256,2048]{2,1,0:T(8,128)(2,1)} %bitcast.19, f32[2,2048]{1,0:T(2,128)S(1)} %collective-permute-done.3, f32[8,2048]{1,0:T(8,128)} %copy-done.6), kind=kLoop, calls=%fused_computation.3 | loop fusion | flops 8192 | bytes 40960 | tf_op jit(solution)/shard_map/dynamic_update_slice | solution.py:458
  83.2 4.3 %all-to-all-done.2 = f32[16,1,17,128]{3,1,2,0:T(1,128)S(1)} async-done(((f32[16,1,17,128]{3,1,2,0:T(1,128)}), f32[16,1,17,128]{3,1,2,0:T(1,128)S(1)}, u32[]{:S(2)}, u32[]{:S(2)}) %all-to-all-start.2) | async-done | bytes 139296 | tf_op jit(solution)/shard_map/all_to_all | solution.py:421
  87.5 0.7 unpack.1
  (2 shorter events, 0.0 us)
Async XLA Ops:
  2.9 22.0 %collective-permute-start = (bf16[144,2048]{1,0:T(8,128)(2,1)S(1)}, bf16[144,2048]{1,0:T(8,128)(2,1)S(1)}, u32[]{:S(2)}, u32[]{:S(2)}) collective-permute-start(bf16[144,2048]{1,0:T(8,128)(2,1)S(1)} %get-tuple-element.26), channel_id=1, source_target_pairs={{0,8},{8,0},{16,24},{24,16},{32,40},{40,32},{48,56},{56,48},{64,72... | collective-permute-start | bytes 1769480 | tf_op jit(solution)/shard_map/ppermute | solution.py:446
  11.7 13.2 %collective-permute-start.2 = (bf16[144,1024]{1,0:T(8,128)(2,1)S(1)}, bf16[144,1024]{1,0:T(8,128)(2,1)S(1)}, u32[]{:S(2)}, u32[]{:S(2)}) collective-permute-start(bf16[144,1024]{1,0:T(8,128)(2,1)S(1)} %get-tuple-element.34), channel_id=1, source_target_pairs={{8,16},{24,32},{40,48},{56,64},{72,80},{88,96},{104,112},{120,128}... | collective-permute-start | bytes 884744 | tf_op jit(solution)/shard_map/ppermute | solution.py:447
  13.6 17.6 %collective-permute-start.1 = (bf16[144,1024]{1,0:T(8,128)(2,1)S(1)}, bf16[144,1024]{1,0:T(8,128)(2,1)S(1)}, u32[]{:S(2)}, u32[]{:S(2)}) collective-permute-start(bf16[144,1024]{1,0:T(8,128)(2,1)S(1)} %get-tuple-element.27), channel_id=1, source_target_pairs={{8,16},{24,32},{40,48},{56,64},{72,80},{88,96},{104,112},{120,128}... | collective-permute-start | bytes 884744 | tf_op jit(solution)/shard_map/ppermute | solution.py:447
  18.2 0.8 copy-start.7
  36.6 1.0 %copy-start = (f32[256,1024]{1,0:T(8,128)}, f32[256,1024]{1,0:T(8,128)S(1)}, u32[]{:S(2)}) copy-start(f32[256,1024]{1,0:T(8,128)S(1)} %get-tuple-element.31.refs_0_) | copy-start | bytes 3145732
  37.6 1.0 %copy-start.2 = (f32[256,1024]{1,0:T(8,128)}, f32[256,1024]{1,0:T(8,128)S(1)}, u32[]{:S(2)}) copy-start(f32[256,1024]{1,0:T(8,128)S(1)} %get-tuple-element.32.refs_1_) | copy-start | bytes 3145732
  38.5 1.0 %copy-start.4 = (f32[256,1024]{1,0:T(8,128)}, f32[256,1024]{1,0:T(8,128)S(1)}, u32[]{:S(2)}) copy-start(f32[256,1024]{1,0:T(8,128)S(1)} %get-tuple-element.33.refs_2_) | copy-start | bytes 3145732
  47.8 26.5 %all-to-all-start.1 = ((f32[32,1,17,128]{3,1,2,0:T(1,128)}), f32[32,1,17,128]{3,1,2,0:T(1,128)S(1)}, u32[]{:S(2)}, u32[]{:S(2)}) async-start(f32[32,1,17,128]{3,1,2,0:T(1,128)} %bitcast.6), calls=%async_computation.1 | async-start | bytes 557056 | tf_op jit(solution)/shard_map/all_to_all | solution.py:421
  62.7 1.2 %copy-start.1 = (f32[256,1024]{1,0:T(8,128)S(1)}, f32[256,1024]{1,0:T(8,128)}, u32[]{:S(2)}) copy-start(f32[256,1024]{1,0:T(8,128)} %copy-done) | copy-start | bytes 3145732
  64.0 1.2 %copy-start.3 = (f32[256,1024]{1,0:T(8,128)S(1)}, f32[256,1024]{1,0:T(8,128)}, u32[]{:S(2)}) copy-start(f32[256,1024]{1,0:T(8,128)} %copy-done.2) | copy-start | bytes 3145732
  65.2 1.2 %copy-start.5 = (f32[256,1024]{1,0:T(8,128)S(1)}, f32[256,1024]{1,0:T(8,128)}, u32[]{:S(2)}) copy-start(f32[256,1024]{1,0:T(8,128)} %copy-done.4) | copy-start | bytes 3145732
  68.9 0.6 copy-start.6
  69.5 12.2 %collective-permute-start.3 = (f32[2,2048]{1,0:T(2,128)S(1)}, f32[2,2048]{1,0:T(2,128)S(1)}, u32[]{:S(2)}, u32[]{:S(2)}) collective-permute-start(f32[2,2048]{1,0:T(2,128)S(1)} %slice.7), channel_id=1, source_target_pairs={{8,0},{16,8},{24,16},{32,24},{40,32},{48,40},{56,48},{64,56},{72,6... | collective-permute-start | bytes 49160 | tf_op jit(solution)/shard_map/ppermute | solution.py:456
  75.1 12.5 %all-to-all-start.2 = ((f32[16,1,17,128]{3,1,2,0:T(1,128)}), f32[16,1,17,128]{3,1,2,0:T(1,128)S(1)}, u32[]{:S(2)}, u32[]{:S(2)}) async-start(f32[16,1,17,128]{3,1,2,0:T(1,128)} %bitcast.8), calls=%async_computation.2 | async-start | bytes 278528 | tf_op jit(solution)/shard_map/all_to_all | solution.py:421
